TPU v7x, 32 devices: a whole 2x2x4 slice. The times are simulated.
32 devices in a mesh: groups: 2 (over y), tensor: 4 (over z), dp: 4 (over x, core).
Axes of the slice: x: 2, y: 2, z: 4, core: 2. Of those that a mesh axis runs over, the one named last changes fastest.
Arguments:
- tokens: bfloat16 [8192, 6144], P(('groups', 'dp'), 'tensor'), parts along dimension 0, may hold values from -6 to 6
- cotangent: bfloat16 [8192, 6144], P(('groups', 'dp'), 'tensor'), parts along dimension 0, may hold values from -6 to 6
- right_in: bfloat16 [64, 96, 384], P('tensor'), may hold values from -0.625 to 0.625
- left_in: bfloat16 [64, 384, 384], P('tensor'), may hold values from -0.3125 to 0.3125
- right_out: bfloat16 [64, 384, 384], P('tensor'), may hold values from -0.3125 to 0.3125
- left_out: bfloat16 [64, 384, 96], P('tensor'), may hold values from -0.3125 to 0.3125
Outputs:
- output: bfloat16 [8192, 6144], P(('groups', 'dp'), 'tensor'), parts along dimension 0
- grad_tokens: bfloat16 [8192, 6144], P(('groups', 'dp'), 'tensor'), parts along dimension 0
- grad_right_in: float32 [128, 96, 384], P(('groups', 'tensor'), None, 'dp'), parts along dimension 0
- grad_left_in: float32 [128, 384, 384], P(('groups', 'tensor'), None, 'dp'), parts along dimension 0
- grad_right_out: float32 [128, 384, 384], P(('groups', 'tensor'), None, 'dp'), parts along dimension 0
- grad_left_out: float32 [128, 384, 96], P(('groups', 'tensor'), 'dp'), parts along dimension 0
There are 2 independent parts, one for each index of `groups`. A program takes and returns all parts, laid end to end along the dimension named above; an argument that names none is the same for every part. Nothing has to cross between parts.
All inputs are finite; a program needn't handle non-finite values.
Results may differ from a plain program's by a relative error of at most 0.0068.
Values may be sent and summed in bfloat16 or wider, within the bound.
No kernel may reach another device: no remote copies, remote signals or barrier semaphores. Data moves between devices by JAX's collectives and lax.ppermute only.
A program may use at most 320 MiB of HBM per device.

v0:
```python
import math

import jax
import jax.numpy as jnp
from jax import lax
from jax.sharding import PartitionSpec as P


def gelu_back(pre, upstream):
    return jax.vjp(jax.nn.gelu, pre)[1](upstream)[0]


def local(tokens, cotangent, right_in, left_in, right_out, left_out):
    f32 = jnp.float32
    bf16 = jnp.bfloat16
    rows = tokens.shape[0]
    local_blocks = right_in.shape[0]
    block_in = right_in.shape[1]
    block_hid = right_in.shape[2]
    all_blocks = local_blocks * lax.axis_size("tensor")
    part_hid = block_hid // all_blocks
    scale = 1.0 / math.sqrt(rows * lax.axis_size("dp"))
    blocks = tokens.reshape(rows, local_blocks, block_in)
    back = cotangent.reshape(rows, local_blocks, block_in)
    ri_split = right_in.reshape(local_blocks, block_in, all_blocks, part_hid)
    first = jnp.einsum("tbi,bics->cbst", blocks, ri_split, preferred_element_type=f32)
    first = first.astype(bf16).reshape(all_blocks, local_blocks * part_hid, rows)
    ro_split = right_out.reshape(local_blocks, block_hid, all_blocks, part_hid)
    arrived_first = lax.all_to_all(first, "tensor", split_axis=0, concat_axis=1, tiled=True)
    count = arrived_first.shape[2]
    pre_act = jnp.einsum("ckt,ckm->cmt", arrived_first, left_in, preferred_element_type=f32)
    hidden_act = jax.nn.gelu(pre_act).astype(bf16)
    second_act = jnp.einsum("cmt,cmds->dcst", hidden_act, ro_split, preferred_element_type=f32)
    second_act = second_act.astype(bf16).reshape(all_blocks, local_blocks * part_hid, count)
    mixed_out = lax.all_to_all(second_act, "tensor", split_axis=0, concat_axis=1, tiled=True)
    output = jnp.einsum("dkt,dkn->tdn", mixed_out, left_out, preferred_element_type=f32)
    output = output.astype(bf16).reshape(rows, local_blocks * block_in)
    grad_lo = jnp.einsum("dkt,tdn->dkn", mixed_out, back, preferred_element_type=f32) * scale
    lo_split = left_out.reshape(local_blocks, all_blocks, part_hid, block_in)
    back_mixed = jnp.einsum("tdn,dcsn->cdst", back, lo_split, preferred_element_type=f32)
    back_mixed = back_mixed.astype(bf16).reshape(all_blocks, local_blocks * part_hid, rows)
    back_second = lax.all_to_all(back_mixed, "tensor", split_axis=0, concat_axis=1, tiled=True)
    grad_ro = (
        jnp.einsum("cmt,cnt->cmn", hidden_act, back_second, preferred_element_type=f32) * scale
    )
    back_hidden = jnp.einsum("cnt,cmn->cmt", back_second, right_out, preferred_element_type=f32)
    back_pre = gelu_back(pre_act, back_hidden).astype(bf16)
    grad_li = (
        jnp.einsum("ckt,cmt->ckm", arrived_first, back_pre, preferred_element_type=f32) * scale
    )
    li_split = left_in.reshape(local_blocks, all_blocks, part_hid, block_hid)
    back_in = jnp.einsum("cmt,cbsm->bcst", back_pre, li_split, preferred_element_type=f32)
    back_in = back_in.astype(bf16).reshape(all_blocks, local_blocks * part_hid, rows)
    back_first = lax.all_to_all(back_in, "tensor", split_axis=0, concat_axis=1, tiled=True)
    grad_x = jnp.einsum("bjt,bij->tbi", back_first, right_in, preferred_element_type=f32)
    grad_tokens = grad_x.astype(bf16).reshape(rows, local_blocks * block_in)
    grad_ri = jnp.einsum("tbi,bjt->bij", blocks, back_first, preferred_element_type=f32) * scale
    grad_ri, grad_li, grad_ro, grad_lo = (
        lax.psum_scatter(grad_ri, "dp", scatter_dimension=2, tiled=True),
        lax.psum_scatter(grad_li, "dp", scatter_dimension=2, tiled=True),
        lax.psum_scatter(grad_ro, "dp", scatter_dimension=2, tiled=True),
        lax.psum_scatter(grad_lo, "dp", scatter_dimension=1, tiled=True),
    )
    return (output, grad_tokens, grad_ri, grad_li, grad_ro, grad_lo)


def solution(mesh):
    placed = (
        P(("groups", "dp"), "tensor"),
        P(("groups", "dp"), "tensor"),
        P("tensor", None, None),
        P("tensor", None, None),
        P("tensor", None, None),
        P("tensor", None, None),
    )
    return jax.shard_map(
        local,
        mesh=mesh,
        in_specs=placed,
        out_specs=(
            P(("groups", "dp"), "tensor"),
            P(("groups", "dp"), "tensor"),
            P(("groups", "tensor"), None, "dp"),
            P(("groups", "tensor"), None, "dp"),
            P(("groups", "tensor"), None, "dp"),
            P(("groups", "tensor"), "dp", None),
        ),
        check_vma=False,
    )
```

profile of v0, /device:TPU:0, one launch (start us, length us, event | category | flops | bytes accessed | tf_op | source)
XLA Modules:
  0.0 1383.2 jit_solution(8253196926471628188)
XLA Ops:
  13.2 9.1 convolution_convert_fusion.1
  22.3 14.6 %copy.85 = bf16[64,96,1024]{2,1,0:T(8,128)(2,1)} copy(bf16[64,96,1024]{2,0,1:T(8,128)(2,1)} %bitcast.122) | data formatting | bytes 25165824 | tf_op jit(solution)/shard_map/reshape | solution.py:27
  36.9 6.3 all-to-all-start
  49.3 9.1 convolution_convert_fusion
  58.4 14.6 %copy.96 = bf16[64,96,1024]{2,1,0:T(8,128)(2,1)} copy(bf16[64,96,1024]{2,0,1:T(8,128)(2,1)} %bitcast.123) | data formatting | bytes 25165824 | tf_op jit(solution)/shard_map/reshape | solution.py:41
  73.0 244.9 %all-to-all-done = bf16[64,96,1024]{2,1,0:T(8,128)(2,1)} async-done(((bf16[64,96,1024]{2,1,0:T(8,128)(2,1)}), bf16[64,96,1024]{2,1,0:T(8,128)(2,1)}, u32[]{:S(2)}, u32[]{:S(2)}) %all-to-all-start) | async-done | bytes 12582944 | tf_op jit(solution)/shard_map/all_to_all | solution.py:29
  317.9 6.8 all-to-all-start.2
  324.7 7.1 copy.88
  331.8 10.9 copy.86
  342.6 16.8 %fusion.27 = f32[16,1024,384]{2,1,0:T(8,128)} fusion(bf16[16,384,1024]{2,1,0:T(8,128)(2,1)} %bitcast.120, bf16[16,384,384]{2,1,0:T(8,128)(2,1)} %param.9), kind=kOutput, calls=%fused_computation.34 | convolution fusion | flops 4831838208 | bytes 42467328 | tf_op jit(solution)/shard_map/ckt,ckm->cmt/dot_general | solution.py:31
  359.4 20.8 %fusion.15 = bf16[16,1024,64,6]{1,2,3,0:T(8,128)(2,1)} fusion(bf16[16,384,64,6]{1,0,3,2:T(8,128)(2,1)} %bitcast.140, f32[16,1024,384]{2,1,0:T(8,128)} %fusion.27), kind=kOutput, calls=%fused_computation.20 | convolution fusion | flops 4894752768 | bytes 42467328 | tf_op jit(solution)/shard_map/cmt,cmds->dcst/dot_general | solution.py:33
  380.2 14.6 %copy.91 = bf16[64,96,1024]{2,1,0:T(8,128)(2,1)} copy(bf16[64,96,1024]{2,0,1:T(8,128)(2,1)} %bitcast.128) | data formatting | bytes 25165824 | tf_op jit(solution)/shard_map/reshape | solution.py:34
  394.8 202.6 %all-to-all-done.2 = bf16[64,96,1024]{2,1,0:T(8,128)(2,1)} async-done(((bf16[64,96,1024]{2,1,0:T(8,128)(2,1)}), bf16[64,96,1024]{2,1,0:T(8,128)(2,1)}, u32[]{:S(2)}, u32[]{:S(2)}) %all-to-all-start.2) | async-done | bytes 12582944 | tf_op jit(solution)/shard_map/all_to_all | solution.py:42
  597.4 6.5 all-to-all-start.1
  603.9 7.4 copy.99
  611.3 10.9 copy.97
  622.2 32.0 %fusion.6 = bf16[16,384,1024]{1,2,0:T(8,128)(2,1)} fusion(f32[16,1024,384]{2,1,0:T(8,128)} %fusion.27, bf16[16,384,1024]{2,1,0:T(8,128)(2,1)} %bitcast.126, bf16[16,384,384]{2,1,0:T(8,128)(2,1)S(1)} %bitcast.139), kind=kOutput, calls=%fused_computation.8 | convolution fusion | flops 4957667328 | bytes 55050240 | tf_op jit(solution)/shard_map/cnt,cmn->cmt/dot_general | solution.py:46
  654.2 13.2 fusion.18
  667.3 14.9 %copy.102 = bf16[64,96,1024]{2,1,0:T(8,128)(2,1)} copy(bf16[64,96,1024]{2,0,1:T(8,128)(2,1)} %bitcast.129) | data formatting | bytes 25165824 | tf_op jit(solution)/shard_map/reshape | solution.py:53
  682.3 194.0 %all-to-all-done.1 = bf16[64,96,1024]{2,1,0:T(8,128)(2,1)} async-done(((bf16[64,96,1024]{2,1,0:T(8,128)(2,1)}), bf16[64,96,1024]{2,1,0:T(8,128)(2,1)}, u32[]{:S(2)}, u32[]{:S(2)}) %all-to-all-start.1) | async-done | bytes 12582944 | tf_op jit(solution)/shard_map/all_to_all | solution.py:35
  876.3 6.3 all-to-all-start.3
  882.7 11.3 copy.92
  894.0 9.8 convolution_multiply_fusion
  909.0 246.1 %all-to-all-done.3 = bf16[64,96,1024]{2,1,0:T(8,128)(2,1)} async-done(((bf16[64,96,1024]{2,1,0:T(8,128)(2,1)}), bf16[64,96,1024]{2,1,0:T(8,128)(2,1)}, u32[]{:S(2)}, u32[]{:S(2)}) %all-to-all-start.3) | async-done | bytes 12582944 | tf_op jit(solution)/shard_map/all_to_all | solution.py:54
  1155.1 11.1 copy.103
  1166.2 9.8 multiply_bitcast_fusion
  1181.3 15.2 %broadcast_multiply_fusion.1 = f32[16,384,384]{1,2,0:T(8,128)} fusion(bf16[16,384,1024]{2,1,0:T(8,128)(2,1)} %bitcast.121, bf16[16,384,1024]{1,2,0:T(8,128)(2,1)} %fusion.6), kind=kOutput, calls=%fused_computation.27 | convolution fusion | flops 4834197504 | bytes 34603008 | tf_op jit(solution)/shard_map/ckt,cmt->ckm/dot_general | solution.py:49
  1196.5 19.2 %broadcast_multiply_fusion = f32[16,384,384]{1,2,0:T(8,128)} fusion(bf16[16,384,1024]{2,1,0:T(8,128)(2,1)} %bitcast.127, f32[16,1024,384]{2,1,0:T(8,128)} %fusion.27), kind=kOutput, calls=%fused_computation.26 | convolution fusion | flops 4890820608 | bytes 47185920 | tf_op jit(solution)/shard_map/cmt,cnt->cmn/dot_general | solution.py:44
  1215.7 7.4 convolution_convert_fusion.3
  1226.1 9.9 convolution_convert_fusion.2
  1244.0 50.9 %reduce-scatter.9.cloned.1.call-done = f32[16,384,96]{1,2,0:T(8,128)} async-done(((f32[16,384,384]{1,2,0:T(8,128)}), f32[16,384,96]{1,2,0:T(8,128)}) %reduce-scatter.9.cloned.1.call-update) | async-done | bytes 2359312 | tf_op jit(solution)/shard_map/reduce_scatter | solution.py:60
  1294.9 81.5 %reduce-scatter.11.cloned.1.call-done = f32[16,384,96]{1,2,0:T(8,128)} async-done(((f32[16,384,384]{1,2,0:T(8,128)}), f32[16,384,96]{1,2,0:T(8,128)}) %reduce-scatter.11.cloned.1.call-update) | async-done | bytes 2359312 | tf_op jit(solution)/shard_map/reduce_scatter | solution.py:61
  (37 shorter events, 33.6 us)
Async XLA Ops:
  13.2 23.7 %copy-start = (bf16[1024,1536]{0,1:T(8,128)(2,1)}, bf16[1024,1536]{0,1:T(8,128)(2,1)S(1)}, u32[]{:S(2)}) copy-start(bf16[1024,1536]{0,1:T(8,128)(2,1)S(1)} %copy.83) | copy-start | bytes 9437188
  36.9 281.0 %all-to-all-start = ((bf16[64,96,1024]{2,1,0:T(8,128)(2,1)}), bf16[64,96,1024]{2,1,0:T(8,128)(2,1)}, u32[]{:S(2)}, u32[]{:S(2)}) async-start(bf16[64,96,1024]{2,1,0:T(8,128)(2,1)} %copy.85), calls=%async_computation | async-start | bytes 25165824 | tf_op jit(solution)/shard_map/all_to_all | solution.py:29
  49.3 23.7 %copy-start.2 = (bf16[1024,1536]{0,1:T(8,128)(2,1)}, bf16[1024,1536]{0,1:T(8,128)(2,1)S(1)}, u32[]{:S(2)}) copy-start(bf16[1024,1536]{0,1:T(8,128)(2,1)S(1)} %copy.94) | copy-start | bytes 9437188
  317.9 279.4 %all-to-all-start.2 = ((bf16[64,96,1024]{2,1,0:T(8,128)(2,1)}), bf16[64,96,1024]{2,1,0:T(8,128)(2,1)}, u32[]{:S(2)}, u32[]{:S(2)}) async-start(bf16[64,96,1024]{2,1,0:T(8,128)(2,1)} %copy.96), calls=%async_computation.2 | async-start | bytes 25165824 | tf_op jit(solution)/shard_map/all_to_all | solution.py:42
  597.4 279.0 %all-to-all-start.1 = ((bf16[64,96,1024]{2,1,0:T(8,128)(2,1)}), bf16[64,96,1024]{2,1,0:T(8,128)(2,1)}, u32[]{:S(2)}, u32[]{:S(2)}) async-start(bf16[64,96,1024]{2,1,0:T(8,128)(2,1)} %copy.91), calls=%async_computation.1 | async-start | bytes 25165824 | tf_op jit(solution)/shard_map/all_to_all | solution.py:35
  603.9 18.3 %slice-start = ((s8[4718592]{0:T(1024)(128)(4,1)}), s8[4194304]{0:T(1024)(128)(4,1)S(1)}, s32[]{:S(2)}) async-start(s8[4718592]{0:T(1024)(128)(4,1)} %bitcast.138), calls=%async_computation.12 | async-start | bytes 8388608
  611.3 10.9 slice-start.1
  876.3 278.8 %all-to-all-start.3 = ((bf16[64,96,1024]{2,1,0:T(8,128)(2,1)}), bf16[64,96,1024]{2,1,0:T(8,128)(2,1)}, u32[]{:S(2)}, u32[]{:S(2)}) async-start(bf16[64,96,1024]{2,1,0:T(8,128)(2,1)} %copy.102), calls=%async_computation.3 | async-start | bytes 25165824 | tf_op jit(solution)/shard_map/all_to_all | solution.py:54
  882.6 356.3 %reduce-scatter.15.cloned.1.call-start = ((), (), s32[]{:S(2)}) async-start(), calls=%async_computation.11 | async-start | bytes 2949120
  882.7 11.3 copy-start.3
  909.0 332.4 %reduce-scatter.13.cloned.1.call-start = ((), (), s32[]{:S(2)}) async-start(), calls=%async_computation.10 | async-start | bytes 2949120
  1155.1 11.1 copy-start.1
  1181.2 113.7 %reduce-scatter.9.cloned.1.call-start = ((), (), s32[]{:S(2)}) async-start(), calls=%async_computation.8 | async-start | bytes 11796480 | tf_op jit(solution)/shard_map/reduce_scatter | solution.py:60
  1196.5 180.0 %reduce-scatter.11.cloned.1.call-start = ((), (), s32[]{:S(2)}) async-start(), calls=%async_computation.9 | async-start | bytes 11796480 | tf_op jit(solution)/shard_map/reduce_scatter | solution.py:61
Sparse Core Ops, SparseCore 0:
  909.1 34.1 reduce-scatter.14
  1181.3 31.9 reduce-scatter.12
  1216.5 78.4 reduce-scatter.8
  1298.0 78.4 reduce-scatter.10
where the time goes:
time: 1390 us; the launch traced here: 1380 us
  waiting for transfers between devices  1020 us (73%)
  matrix products  172 us (12%)
  local copies, waits for them, and re-layouts  151 us (11%)
  starting transfers between devices  26 us (2%)
  between operations  14.1 us (1%)
    all_to_all x1, waiting for transfers between devices, local(): lax.all_to_all(back_in, 'tensor', split_axis=0, concat_axis=1, tiled=True)  246 us
    all_to_all x1, waiting for transfers between devices, local(): lax.all_to_all(first, 'tensor', split_axis=0, concat_axis=1, tiled=True)  245 us
    all_to_all x1, waiting for transfers between devices, local(): lax.all_to_all(back_mixed, 'tensor', split_axis=0, concat_axis=1, tiled=T...  203 us
    all_to_all x1, waiting for transfers between devices, local(): lax.all_to_all(second_act, 'tensor', split_axis=0, concat_axis=1, tiled=T...  194 us
    reduce_scatter x1, waiting for transfers between devices, local(): lax.psum_scatter(grad_ro, 'dp', scatter_dimension=2, tiled=True)  81.5 us
    reduce_scatter x1, waiting for transfers between devices, local(): lax.psum_scatter(grad_li, 'dp', scatter_dimension=2, tiled=True)  50.9 us
    unnamed x28, local copies, waits for them, and re-layouts  47.8 us
    dot_general x1, matrix products, local(): jnp.einsum('cnt,cmn->cmt', back_second, right_out, preferred_element_type...  32 us
  transfers between devices with their start and end apart: 8, of which 6 were waited for; matrix products, arithmetic and copies ran while one was open for 21% of the time, Pallas kernels for 0%

commit v1 on v0

--- a/solution.py
+++ b/solution.py
@@ -1,16 +1,425 @@
+import functools
 import math
 
 import jax
 import jax.numpy as jnp
 from jax import lax
+from jax.experimental import pallas as pl
+from jax.experimental.pallas import tpu as pltpu
+from jax.sharding import Mesh
 from jax.sharding import PartitionSpec as P
+
+F32 = jnp.float32
+BF16 = jnp.bfloat16
+PACK = 8
+TAIL = 4
+LANES = 128
+VMEM = 56 * 1024 * 1024
+
+
+def dot(a, b, contract):
+    return lax.dot_general(a, b, ((contract[:1], contract[1:]), ((), ())), preferred_element_type=F32)
+
+
+def scratch(blocks, rows, lanes):
+    return pltpu.VMEM((lanes // LANES, blocks * (rows + 1), LANES), F32)
+
+
+def spread_kernel(steps, blocks, part, pos_ref, *refs):
+    *act_refs, w_ref, out_ref, buf = refs
+    step = pl.program_id(0)
+    wide, rows = w_ref.shape[2:]
+    tiles = act_refs[0].shape[1] // LANES
+    pitch = rows + 1
+
+    @pl.when(step < steps)
+    def _():
+        at = pl.ds(pl.multiple_of(step * PACK * pitch, 8), PACK * pitch)
+        for p in range(PACK):
+            for n, ref in enumerate(act_refs):
+                first = dot(w_ref[p, 0], ref[0, :, p * wide : (p + 1) * wide], (0, 1))
+                for k in range(tiles):
+                    buf.at[n * tiles + k, at, :][p * pitch : p * pitch + rows, :] = first[:, k * LANES : (k + 1) * LANES]
+
+    @pl.when(step >= steps)
+    def _():
+        for p in range(TAIL):
+            c = (step - steps) * TAIL + p
+            for s in range(part):
+                for k in range(buf.shape[0]):
+                    rest = buf[k, pl.ds(c * part + s, blocks, stride=pitch), :]
+                    out_ref[p, s * blocks : (s + 1) * blocks, k * LANES : (k + 1) * LANES] = rest.astype(BF16)
+
+
+def spread(pos, acts, w, which, part):
+    blocks, _, wide, rows = w.shape
+    quarters, count, span = acts[0].shape
+    lanes = count * len(acts)
+    steps = blocks // PACK
+    per = span // (PACK * wide)
+    own_c = rows // part
+
+    def act_map(i, pos):
+        j = jnp.minimum(i, steps - 1)
+        return j // per, 0, lax.rem(j, per)
+
+    def w_map(i, pos):
+        j = jnp.minimum(i, steps - 1)
+        return lax.rem(j // per + 4 - pos[0], 4) * per + lax.rem(j, per), which, 0, 0
+
+    return pl.pallas_call(
+        functools.partial(spread_kernel, steps, blocks, part),
+        grid_spec=pltpu.PrefetchScalarGridSpec(
+            num_scalar_prefetch=1,
+            grid=(steps + own_c // TAIL,),
+            in_specs=[pl.BlockSpec((1, count, PACK * wide), act_map)] * len(acts) + [pl.BlockSpec((PACK, 1, wide, rows), w_map)],
+            out_specs=pl.BlockSpec((TAIL, blocks * part, lanes), lambda i, pos: (jnp.maximum(i - steps, 0), 0, 0)),
+            scratch_shapes=[scratch(blocks, rows, lanes)],
+        ),
+        out_shape=jax.ShapeDtypeStruct((own_c, blocks * part, lanes), BF16),
+        compiler_params=pltpu.CompilerParams(vmem_limit_bytes=VMEM),
+        cost_estimate=pl.CostEstimate(flops=2 * blocks * rows * wide * lanes, bytes_accessed=58_000_000, transcendentals=0),
+        name="spread",
+    )(pos, *acts, w)
+
+
+def gather_kernel(lead, blocks, part, pos_ref, mixed_ref, *refs):
+    *act_refs, w_ref, keep_ref, send_ref, grad_ref, buf = refs
+    step = pl.program_id(0)
+    wide, rows = w_ref.shape[2:]
+    count = act_refs[0].shape[1]
+    pitch = rows + 1
+
+    @pl.when(step < lead)
+    def _():
+        for p in range(TAIL):
+            c = step * TAIL + p
+            for s in range(part):
+                for k in range(buf.shape[0]):
+                    rest = mixed_ref[p, s * blocks : (s + 1) * blocks, k * LANES : (k + 1) * LANES]
+                    buf[k, pl.ds(c * part + s, blocks, stride=pitch), :] = rest.astype(F32)
+
+    @pl.when(step >= lead)
+    def _():
+        quarter_steps = (blocks // PACK) // 4
+        r = (step - lead) // quarter_steps
+        t = lax.rem(r + pos_ref[0], 4)
+        group = t * quarter_steps + lax.rem(step - lead, quarter_steps)
+        at = pl.ds(pl.multiple_of(group * PACK * pitch, 8), PACK * pitch)
+        outs = []
+        for p in range(PACK):
+            tiles = [buf.at[k, at, :][p * pitch : p * pitch + rows, :].astype(BF16) for k in range(buf.shape[0])]
+            z = jnp.concatenate(tiles, axis=1)
+            outs.append(dot(w_ref[p, 0], z, (1, 0)))
+            g = 0.0
+            for n, ref in enumerate(act_refs):
+                g = g + dot(z[:, n * count : (n + 1) * count], ref[0, :, p * wide : (p + 1) * wide], (1, 0))
+            top, left = divmod(p, PACK // 2)
+            grad_ref[0, top, :, left * wide : (left + 1) * wide] = g.astype(BF16)
+        out = jnp.concatenate(outs, axis=0).T.astype(BF16)
+        for n in range(len(act_refs)):
+            ref = keep_ref if n < len(act_refs) // 2 else send_ref
+            ref[n % (len(act_refs) // 2), 0] = out[n * count : (n + 1) * count]
+
+
+def gather(pos, mixed, acts, w, which, part):
+    blocks, _, wide, rows = w.shape
+    quarters, count, span = acts[0].shape
+    half = len(acts) // 2
+    lanes = count * len(acts)
+    per = span // (PACK * wide)
+    own_c = rows // part
+    lead = own_c // TAIL
+    steps = blocks // PACK
+
+    def place(i, pos):
+        j = jnp.maximum(i - lead, 0)
+        return lax.rem(j // per + pos[0], 4), lax.rem(j, per)
+
+    def act_map(i, pos):
+        t, k = place(i, pos)
+        return t, 0, k
+
+    def out_map(i, pos):
+        t, k = place(i, pos)
+        return 0, t, 0, k
+
+    act = pl.BlockSpec((1, count, PACK * wide), act_map)
+    out = pl.BlockSpec((half, 1, count, PACK * wide), out_map)
+    return pl.pallas_call(
+        functools.partial(gather_kernel, lead, blocks, part),
+        grid_spec=pltpu.PrefetchScalarGridSpec(
+            num_scalar_prefetch=1,
+            grid=(lead + steps,),
+            in_specs=[pl.BlockSpec((TAIL, blocks * part, lanes), lambda i, pos: (jnp.minimum(i, lead - 1), 0, 0))]
+            + [act] * len(acts)
+            + [pl.BlockSpec((PACK, 1, wide, rows), lambda i, pos: (jnp.maximum(i - lead, 0), which, 0, 0))],
+            out_specs=[out, out, pl.BlockSpec((1, 2, rows, PACK // 2 * wide), lambda i, pos: (jnp.maximum(i - lead, 0), 0, 0, 0))],
+            scratch_shapes=[scratch(blocks, rows, lanes)],
+        ),
+        out_shape=[jax.ShapeDtypeStruct((half, quarters, count, span), BF16)] * 2
+        + [jax.ShapeDtypeStruct((steps, 2, rows, PACK // 2 * wide), BF16)],
+        compiler_params=pltpu.CompilerParams(vmem_limit_bytes=VMEM),
+        cost_estimate=pl.CostEstimate(flops=4 * blocks * rows * wide * lanes, bytes_accessed=76_000_000, transcendentals=0),
+        name="gather",
+    )(pos, mixed, *acts, w)
+
+
+K0 = math.sqrt(2.0 / math.pi)
+
+
+def forward_kernel(at_ref, wat_ref, m_ref, li_ref, ro_ref, *refs):
+    out_ref = refs[-1]
+    pre = dot(li_ref[0, 0], m_ref[0], (0, 0))
+    hidden = pre * (0.5 * (1.0 + jnp.tanh(K0 * (pre + 0.044715 * (pre * pre * pre)))))
+    out_ref[0] = dot(ro_ref[0, 0], hidden.astype(BF16), (0, 0)).astype(BF16)
+
+
+def forward(at, wat, mixed, w, second):
+    count = at.shape[0]
+    _, hid, tokens = mixed.shape
+    act = pl.BlockSpec((1, hid, tokens), lambda i, at, wat: (at[i], 0, 0))
+    old = [] if second is None else [second]
+    return pl.pallas_call(
+        forward_kernel,
+        grid_spec=pltpu.PrefetchScalarGridSpec(
+            num_scalar_prefetch=2,
+            grid=(count,),
+            in_specs=[
+                act,
+                pl.BlockSpec((1, 1, hid, hid), lambda i, at, wat: (wat[i], 0, 0, 0)),
+                pl.BlockSpec((1, 1, hid, hid), lambda i, at, wat: (wat[i], 1, 0, 0)),
+            ]
+            + [pl.BlockSpec(memory_space=pl.ANY)] * len(old),
+            out_specs=act,
+        ),
+        out_shape=jax.ShapeDtypeStruct(mixed.shape, BF16),
+        input_output_aliases={5: 0} if old else {},
+        compiler_params=pltpu.CompilerParams(vmem_limit_bytes=VMEM),
+        cost_estimate=pl.CostEstimate(flops=4 * count * hid * hid * tokens, bytes_accessed=count * 8_000_000, transcendentals=0),
+        name="forward",
+    )(at, wat, mixed, w, w, *old)
+
+
+def backward_kernel(blocks, at_ref, wat_ref, m_ref, b_ref, li_ref, ro_ref, b_out, grad_ref, bp):
+    m = m_ref[0]
+    li = li_ref[0, 0]
+    pre = dot(li, m, (0, 0))
+    square = pre * pre
+    th = jnp.tanh(K0 * (pre * (1.0 + 0.044715 * square)))
+    cdf = 0.5 * (1.0 + th)
+    hidden = (pre * cdf).astype(BF16)
+    slope = cdf + pre * (0.5 * K0) * (1.0 - th * th) * (1.0 + (3.0 * 0.044715) * square)
+    bp[...] = (dot(ro_ref[0, 0], b_ref[0], (1, 0)) * slope).astype(BF16)
+    b_out[0] = dot(li, bp[...], (1, 0)).astype(BF16)
+    g_li = dot(bp[...], m, (1, 1)).astype(BF16)
+    g_ro = dot(b_ref[0], hidden, (1, 1)).astype(BF16)
+    chunks, rows = grad_ref.shape[2:4]
+    piece = blocks // chunks
+    for q in range(chunks):
+        grad_ref[0, 0, q] = g_li[q * rows : (q + 1) * rows]
+        for s in range(rows // piece):
+            start = s * blocks + q * piece
+            grad_ref[0, 1, q, s * piece : (s + 1) * piece, :] = g_ro[start : start + piece]
+
+
+def backward(at, wat, mixed, back, w, blocks):
+    count = at.shape[0]
+    _, hid, tokens = mixed.shape
+    act = pl.BlockSpec((1, hid, tokens), lambda i, at, wat: (at[i], 0, 0))
+    return pl.pallas_call(
+        functools.partial(backward_kernel, blocks),
+        grid_spec=pltpu.PrefetchScalarGridSpec(
+            num_scalar_prefetch=2,
+            grid=(count,),
+            in_specs=[
+                act,
+                act,
+                pl.BlockSpec((1, 1, hid, hid), lambda i, at, wat: (wat[i], 0, 0, 0)),
+                pl.BlockSpec((1, 1, hid, hid), lambda i, at, wat: (wat[i], 1, 0, 0)),
+            ],
+            out_specs=[act, pl.BlockSpec((1, 2, 4, hid // 4, hid), lambda i, at, wat: (i, 0, 0, 0, 0))],
+            scratch_shapes=[pltpu.VMEM((hid, tokens), BF16)],
+        ),
+        out_shape=[jax.ShapeDtypeStruct(mixed.shape, BF16), jax.ShapeDtypeStruct((count, 2, 4, hid // 4, hid), BF16)],
+        input_output_aliases={3: 0},
+        compiler_params=pltpu.CompilerParams(vmem_limit_bytes=VMEM),
+        cost_estimate=pl.CostEstimate(flops=10 * count * hid * hid * tokens, bytes_accessed=count * 15_000_000, transcendentals=0),
+        name="backward",
+    )(at, wat, mixed, back, w, w)
+
+
+def swap(a, axis):
+    return lax.ppermute(a, axis, [(0, 1), (1, 0)])
+
+
+def after(value, *others):
+    return lax.optimization_barrier((value, *others))[0]
+
+
+def up(a, first, last):
+    return lax.ppermute(a, "tensor", [(i, i + 1) for i in range(first, last)])
+
+
+def down(a, first, last):
+    return lax.ppermute(a, "tensor", [(i, i - 1) for i in range(first, last, -1)])
+
+
+def add(*terms):
+    total = terms[0].astype(F32)
+    for term in terms[1:]:
+        total = total + term.astype(F32)
+    return total
+
+
+def all_to_all(a):
+    return lax.all_to_all(a, "tensor", split_axis=0, concat_axis=0, tiled=True)
+
+
+def tokens_plan(tokens, cotangent, right_in, left_in, right_out, left_out):
+    g = lax.axis_index("groups")
+    z = lax.axis_index("tensor")
+    x = lax.axis_index("x")
+    core = lax.axis_index("core")
+    mate = 2 * x + core
+    rows, span = tokens.shape
+    nb, wide, hid = right_in.shape
+    blocks = 4 * nb
+    part = hid // blocks
+    own_nb = nb // 4
+    scale = 1.0 / math.sqrt(rows * 4)
+    pos = jnp.stack([z, x]).astype(jnp.int32)
+
+    place = jnp.arange(hid)
+    reorder = (place[:, None] % blocks * part + place[:, None] // blocks == place[None, :]).astype(BF16)
+
+    def line_gather(a):
+        u1, d1 = up(a, 0, 3), down(a, 3, 0)
+        u2, d2 = up(u1, 1, 3), down(d1, 2, 0)
+        u3, d3 = up(u2, 2, 3), down(d2, 1, 0)
+        return jnp.stack([jnp.where(z == 3, u3, d1), jnp.where(z < 2, d2, u2), jnp.where(z == 0, d3, u1)])
+
+    def by_group(a, b):
+        return jnp.where(g == 0, jnp.stack([a, b], axis=1), jnp.stack([b, a], axis=1))
+
+    small = jnp.stack([right_in, jnp.swapaxes(left_out, 1, 2)], axis=1)
+    small = small.reshape(nb, 2, wide, 4, 4, own_nb * part)
+    small = lax.dynamic_index_in_dim(small, mate, axis=4, keepdims=False).reshape(nb, 2, wide, hid // 4)
+    fs = line_gather(lax.dynamic_slice_in_dim(small, g * (nb // 2), nb // 2, axis=0))
+
+    own_li = lax.dynamic_slice_in_dim(left_in, mate * own_nb, own_nb, axis=0)
+    own_ro = lax.dynamic_slice_in_dim(right_out, mate * own_nb, own_nb, axis=0)
+    own_li = jnp.einsum("pk,ckm->cpm", reorder, own_li, preferred_element_type=F32).astype(BF16)
+    own_ro = jnp.einsum("cmn,pn->cmp", own_ro, reorder, preferred_element_type=F32).astype(BF16)
+    own_w = jnp.stack([own_li, own_ro], axis=1)
+
+    own_x = all_to_all(tokens.reshape(4, rows // 4, span))
+    x_x = swap(own_x, "x")
+    cotangent, mine, own_x, fs = lax.optimization_barrier((cotangent, lax.dynamic_slice_in_dim(own_w, 2 * g, 2, axis=0), own_x, fs))
+    own_y = all_to_all(cotangent.reshape(4, rows // 4, span))
+    acts_x = [own_x, x_x, swap(own_x, "core"), swap(x_x, "core")]
+    f = line_gather(mine)
+    yf = swap(f, "groups")
+    x_y = swap(own_y, "x")
+    small = jnp.concatenate([small, by_group(fs, swap(fs, "groups")).reshape(3 * nb, *small.shape[1:])])
+
+    order = [(gr, h) for gr in range(2) for h in range(2)]
+    index = {(gr, h): 2 * ((g + gr) % 2) + h for gr, h in order}
+    six = jnp.arange(6, dtype=jnp.int32)
+    pieces = [
+        (jnp.stack([z * own_nb + index[o] for o in order]).astype(jnp.int32), jnp.stack([index[o] for o in order]).astype(jnp.int32), own_w)
+    ]
+    for gr, w in enumerate((f, yf)):
+        at = [(z + r) % 4 * own_nb + index[gr, h] for r in (1, 2, 3) for h in range(2)]
+        pieces.append((jnp.stack(at).astype(jnp.int32), six, w.reshape(6, 2, hid, hid)))
+
+    mixed = spread(pos, acts_x, small, 0, part)
+    second = None
+    for at, wat, w in pieces:
+        if w is pieces[2][2]:
+            second, x_y = lax.optimization_barrier((second, x_y))
+        second = forward(at, wat, mixed, w, second)
+    acts_y = [own_y, x_y, swap(own_y, "core"), swap(x_y, "core")]
+    keep, send, lo = gather(pos, second, acts_y, small, 1, part)
+    got = swap(send, "core")
+    back = spread(pos, acts_y, small, 1, part)
+    back, got = lax.optimization_barrier((back, got))
+    out_x = swap(add(keep[1], got[1]).astype(BF16), "x")
+    out = add(keep[0], got[0])
+
+    grads = {}
+
+    def step(n):
+        at, wat, w = pieces[n]
+        return backward(at, wat, mixed, back, w, blocks)
+
+    def shares(n, first):
+        first = first.reshape(4, -1, hid // 4, hid)
+        by_place = grads[n].reshape(3, -1, hid // 4, hid)
+        return [jnp.concatenate([by_place[r], first[r + 1]]) for r in range(3)]
+
+    def first_hop(s):
+        return up(s[2], 0, 1), down(s[0], 3, 2)
+
+    def second_hop(s, u, d):
+        return up(add(s[1], u).astype(BF16), 0, 2), down(add(s[1], d).astype(BF16), 3, 1)
+
+    def third_hop(s, u, d):
+        return up(add(s[0], u).astype(BF16), 0, 3), down(add(s[2], d).astype(BF16), 3, 0)
+
+    back, grads[1] = step(1)
+    s1 = shares(1, lo)
+    u, d = first_hop(s1)
+    back, grads[2] = step(2)
+    back, u, d = lax.optimization_barrier((back, u, d))
+    u, d = second_hop(s1, u, d)
+    back, grads[0] = step(0)
+    back, out_x, u, d = lax.optimization_barrier((back, out_x, u, d))
+    output = all_to_all(add(out, out_x).astype(BF16)).reshape(rows, span)
+    u1, d1 = third_hop(s1, u, d)
+    keep, send, ri = gather(pos, back, acts_x, small, 0, part)
+    got = swap(send, "core")
+    gx_x = swap(add(keep[1], got[1]).astype(BF16), "x")
+    s2 = shares(2, ri)
+    u, d = first_hop(s2)
+    u, d = second_hop(s2, u, d)
+    u, d, gx_x = lax.optimization_barrier((u, d, gx_x))
+    grad_tokens = all_to_all(add(add(keep[0], got[0]), gx_x).astype(BF16)).reshape(rows, span)
+    v1, e1 = third_hop(s2, u, d)
+
+    def reduced(n, first, u1, d1):
+        own = grads[0].reshape(2, -1, hid // 4, hid)[n - 1]
+        count = own.shape[0]
+        total = add(jnp.concatenate([own, first.reshape(4, -1, hid // 4, hid)[0]]), u1, d1).astype(BF16)
+        second = total[:count].reshape(-1, 2, 2, hid // 4, hid).transpose(1, 2, 0, 3, 4).reshape(2, 2, -1, hid)
+        first = total[count:].reshape(-1, 2, 2, hid // 16, hid).transpose(1, 2, 0, 3, 4).reshape(2, 2, -1, hid)
+        total = jnp.concatenate([second, first], axis=2)
+        kept = lax.dynamic_index_in_dim(total, x, axis=0, keepdims=False)
+        got = swap(lax.dynamic_index_in_dim(total, 1 - x, axis=0, keepdims=False), "x")
+        total = jnp.where(x == 0, jnp.stack([kept, got], axis=1), jnp.stack([got, kept], axis=1))
+        kept = lax.dynamic_index_in_dim(total, core, axis=0, keepdims=False)
+        got = swap(lax.dynamic_index_in_dim(total, 1 - core, axis=0, keepdims=False), "core")
+        total = jnp.where(core == 0, jnp.stack([kept, got], axis=1), jnp.stack([got, kept], axis=1)).reshape(4, -1, hid)
+        cut = second.shape[2]
+        return total[:, :cut].reshape(4, 2, 2, hid // 4, hid), total[:, cut:].reshape(4, nb // PACK, 2, hid // 16, PACK // 2, wide)
+
+    big0, grad_lo = reduced(1, lo, u1, d1)
+    big1, grad_ri = reduced(2, ri, v1, e1)
+    big = by_group(big0, big1).reshape(nb, 2, hid // 4, hid)
+    grad_li = jnp.einsum("cmp,pk->cmk", big[:, 0], reorder, preferred_element_type=F32) * scale
+    grad_li = jnp.swapaxes(grad_li, 1, 2)
+    grad_ro = big[:, 1].reshape(nb, part, blocks // 4, hid).swapaxes(1, 2).reshape(nb, hid // 4, hid).astype(F32) * scale
+    grad_ro = jnp.swapaxes(grad_ro, 1, 2)
+    grad_lo = grad_lo.astype(F32).transpose(1, 2, 4, 0, 3, 5).reshape(nb, hid // 4, wide) * scale
+    grad_ri = grad_ri.astype(F32).transpose(1, 2, 4, 5, 0, 3).reshape(nb, wide, hid // 4) * scale
+    return (output, grad_tokens, grad_ri, grad_li, grad_ro, grad_lo)
 
 
 def gelu_back(pre, upstream):
     return jax.vjp(jax.nn.gelu, pre)[1](upstream)[0]
 
 
-def local(tokens, cotangent, right_in, left_in, right_out, left_out):
+def blocks_plan(tokens, cotangent, right_in, left_in, right_out, left_out):
     f32 = jnp.float32
     bf16 = jnp.bfloat16
     rows = tokens.shape[0]
@@ -65,25 +474,19 @@
 
 
 def solution(mesh):
-    placed = (
-        P(("groups", "dp"), "tensor"),
-        P(("groups", "dp"), "tensor"),
-        P("tensor", None, None),
-        P("tensor", None, None),
-        P("tensor", None, None),
-        P("tensor", None, None),
-    )
+    wide = mesh.shape["tensor"] == 4 and mesh.shape["dp"] == 4 and mesh.shape["groups"] == 2
+    dp = "dp"
+    if wide:
+        dp = ("x", "core")
+        mesh = Mesh(mesh.devices.reshape(2, 4, 2, 2), ("groups", "tensor", *dp))
+    row = ("groups", "x", "core") if wide else ("groups", "dp")
+    acts = P(row, "tensor")
+    placed = (acts, acts, P("tensor", None, None), P("tensor", None, None), P("tensor", None, None), P("tensor", None, None))
+    own = ("groups", "tensor")
     return jax.shard_map(
-        local,
+        tokens_plan if wide else blocks_plan,
         mesh=mesh,
         in_specs=placed,
-        out_specs=(
-            P(("groups", "dp"), "tensor"),
-            P(("groups", "dp"), "tensor"),
-            P(("groups", "tensor"), None, "dp"),
-            P(("groups", "tensor"), None, "dp"),
-            P(("groups", "tensor"), None, "dp"),
-            P(("groups", "tensor"), "dp", None),
-        ),
+        out_specs=(acts, acts, P(own, None, dp), P(own, None, dp), P(own, None, dp), P(own, dp, None)),
         check_vma=False,
     )

time: 1390 us -> 805 us (0.58)
  waiting for transfers between devices: 1020 us -> 398 us
  Pallas kernels: 0 us -> 167 us
  matrix products: 172 us -> 8.01 us
  local copies, waits for them, and re-layouts: 151 us -> 48.6 us
  other arithmetic: 0.01 us -> 74.3 us
  starting transfers between devices: 26 us -> 98.9 us
    all_to_all x4, waiting for transfers between devices: 888 us -> 15.5 us  [all_to_all(): return lax.all_to_all(a, 'tensor', split_axis=0, concat_axis=0, tiled=True)]
    ppermute x0 -> x40, waiting for transfers between devices: none -> 382 us  [the longest x12 179 us: up(): return lax.ppermute(a, 'tensor', [(i, i + 1) for i in range(first, last)])]
    pallas_call x0 -> x10, Pallas kernels: none -> 167 us  [the longest x2 52.2 us: gather(): pl.pallas_call(functools.partial(gather_kernel, lead, blocks, part), grid...]
    dot_general x12 -> x3, matrix products: 172 us -> 8.01 us  [the longest x1 3.66 us: tokens_plan(): jnp.einsum('cmp,pk->cmk', big[:, 0], reorder, preferred_element_type=F32)]
    reduce_scatter x2 -> x0, waiting for transfers between devices: 132 us -> none  [the longest x1 81.5 us: local(): lax.psum_scatter(grad_ro, 'dp', scatter_dimension=2, tiled=True)]
    ppermute x0 -> x40, starting transfers between devices: none -> 76.8 us  [the longest x12 47.4 us: up(): return lax.ppermute(a, 'tensor', [(i, i + 1) for i in range(first, last)])]
    reshape x4 -> x1, local copies, waits for them, and re-layouts: 58.7 us -> 1.16 us  [tokens_plan(): lax.dynamic_index_in_dim(small, mate, axis=4, keepdims=False)]
    all_to_all x4 -> x0, local copies, waits for them, and re-layouts: 44.1 us -> none  [the longest x1 11.3 us: local(): lax.all_to_all(second_act, 'tensor', split_axis=0, concat_axis=1, tiled=T...]
  transfers between devices with their start and end apart: 8 -> 44, of which waited for: 6 -> 17; matrix products, arithmetic and copies ran while one was open for 21% -> 15% of each run, Pallas kernels for 0% -> 12%
where the time goes in v1:
time: 805 us; the launch traced here: 797 us
  waiting for transfers between devices  398 us (49%)
  Pallas kernels  167 us (21%)
  starting transfers between devices  98.9 us (12%)
  other arithmetic  74.3 us (9%)
  local copies, waits for them, and re-layouts  48.6 us (6%)
    ppermute x12, waiting for transfers between devices, up(): return lax.ppermute(a, 'tensor', [(i, i + 1) for i in range(first, last)])  179 us
    ppermute x12, waiting for transfers between devices, down(): lax.ppermute(a, 'tensor', [(i, i - 1) for i in range(first, last, -1)])  131 us
    ppermute x16, waiting for transfers between devices, swap(): return lax.ppermute(a, axis, [(0, 1), (1, 0)])  71.8 us
    pallas_call x2, Pallas kernels, gather(): pl.pallas_call(functools.partial(gather_kernel, lead, blocks, part), grid...  52.2 us
    pallas_call x3, Pallas kernels, backward(): pl.pallas_call(functools.partial(backward_kernel, blocks), grid_spec=pltp...  49.6 us
    ppermute x12, starting transfers between devices, up(): return lax.ppermute(a, 'tensor', [(i, i + 1) for i in range(first, last)])  47.4 us
    pallas_call x2, Pallas kernels, spread(): pl.pallas_call(functools.partial(spread_kernel, steps, blocks, part), gri...  36 us
    pallas_call x3, Pallas kernels, forward(): pl.pallas_call(forward_kernel, grid_spec=pltpu.PrefetchScalarGridSpec(num...  29.7 us
  transfers between devices with their start and end apart: 44, of which 17 were waited for; matrix products, arithmetic and copies ran while one was open for 15% of the time, Pallas kernels for 12%

profile of v1, /device:TPU:0, one launch (start us, length us, event | category | flops | bytes accessed | tf_op | source)
XLA Modules:
  0.0 796.6 jit_solution(7008958332472249050)
XLA Ops:
  0.6 6.5 all-to-all-start
  15.5 50.8 %collective-permute-done = bf16[8,2,96,96]{2,3,1,0:T(8,128)(2,1)S(1)} collective-permute-done((bf16[8,2,96,96]{2,3,1,0:T(8,128)(2,1)S(1)}, bf16[8,2,96,96]{2,3,1,0:T(8,128)(2,1)S(1)}, u32[]{:S(2)}, u32[]{:S(2)}) %collective-permute-start) | collective-permute-done | bytes 294944 | tf_op jit(solution)/shard_map/ppermute | solution.py:261
  76.0 26.0 %collective-permute-done.4 = bf16[8,2,96,96]{2,3,1,0:T(8,128)(2,1)} collective-permute-done((bf16[8,2,96,96]{2,3,1,0:T(8,128)(2,1)}, bf16[8,2,96,96]{2,3,1,0:T(8,128)(2,1)}, u32[]{:S(2)}, u32[]{:S(2)}) %collective-permute-start.4) | collective-permute-done | bytes 294944 | tf_op jit(solution)/shard_map/ppermute | solution.py:265
  105.4 7.4 collective-permute-done.5
  127.2 67.1 %collective-permute-done.13 = bf16[2,2,384,384]{3,2,1,0:T(8,128)(2,1)} collective-permute-done((bf16[2,2,384,384]{3,2,1,0:T(8,128)(2,1)}, bf16[2,2,384,384]{3,2,1,0:T(8,128)(2,1)}, u32[]{:S(2)}, u32[]{:S(2)}) %collective-permute-start.13) | collective-permute-done | bytes 1179680 | tf_op jit(solution)/shard_map/ppermute | solution.py:265
  199.4 22.5 %collective-permute-done.9 = bf16[3,8,2,96,96]{3,4,2,1,0:T(8,128)(2,1)} collective-permute-done((bf16[3,8,2,96,96]{3,4,2,1,0:T(8,128)(2,1)}, bf16[3,8,2,96,96]{3,4,2,1,0:T(8,128)(2,1)}, u32[]{:S(2)}, u32[]{:S(2)}) %collective-permute-start.9) | collective-permute-done | bytes 884768 | tf_op jit(solution)/shard_map/ppermute | solution.py:253
  223.5 16.6 %collective-permute-done.14 = bf16[2,2,384,384]{3,2,1,0:T(8,128)(2,1)} collective-permute-done((bf16[2,2,384,384]{3,2,1,0:T(8,128)(2,1)}, bf16[2,2,384,384]{3,2,1,0:T(8,128)(2,1)}, u32[]{:S(2)}, u32[]{:S(2)}) %collective-permute-start.14) | collective-permute-done | bytes 1179680 | tf_op jit(solution)/shard_map/ppermute | solution.py:265
  254.9 14.0 %collective-permute-done.15 = bf16[2,2,384,384]{3,2,1,0:T(8,128)(2,1)} collective-permute-done((bf16[2,2,384,384]{3,2,1,0:T(8,128)(2,1)}, bf16[2,2,384,384]{3,2,1,0:T(8,128)(2,1)}, u32[]{:S(2)}, u32[]{:S(2)}) %collective-permute-start.15) | collective-permute-done | bytes 1179680 | tf_op jit(solution)/shard_map/ppermute | solution.py:265
  276.9 17.9 %spread.2.m_ref = bf16[16,384,1024]{2,1,0:T(8,128)(2,1)} custom-call(s32[2]{0:T(128)} %pad_add_fusion.pos_ref, bf16[4,256,1536]{2,1,0:T(8,128)(2,1)} %all-to-all-done.refs_0_, bf16[4,256,1536]{2,1,0:T(8,128)(2,1)} %collective-permute-done.6.refs_1_, bf16[4,256,1536]{2,1,0:T(8,128)(2,1)} %collective-permute-done.7.refs_2_, ...), custom_call_target="tpu_custom_call" | custom-call | flops 1207959552 | bytes 58000000 | tf_op jit(solution)/shard_map/spread/pallas_call | solution.py:70
  294.8 8.0 %forward.3.refs_0_ = bf16[16,384,1024]{2,1,0:T(8,128)(2,1)} custom-call(s32[4]{0:T(128)} %get-tuple-element.106.at_ref, s32[4]{0:T(128)} %get-tuple-element.107.wat_ref, bf16[16,384,1024]{2,1,0:T(8,128)(2,1)} %spread.2.m_ref, bf16[4,2,384,384]{3,2,1,0:T(8,128)(2,1)} %pad_maximum_fusion.2.li_ref.ro_ref, bf16[4,2,384,384]{3,2,1,0:T(8,128)(2,1)} %pad_maximum_fusion.2.li_ref.ro_ref), custom_call_target="tpu_custom_call" | custom-call | flops 2415919104 | bytes 32000000 | tf_op jit(solution)/shard_map/forward/pallas_call | solution.py:183
  303.4 10.9 %forward.4.refs_0_ = bf16[16,384,1024]{2,1,0:T(8,128)(2,1)} custom-call(s32[6]{0:T(128)} %stack.233.at_ref, s32[6]{0:T(128)} %iota.23.wat_ref, bf16[16,384,1024]{2,1,0:T(8,128)(2,1)} %spread.2.m_ref, bf16[6,2,384,384]{3,2,1,0:T(8,128)(2,1)} %bitcast.143, bf16[6,2,384,384]{3,2,1,0:T(8,128)(2,1)} %bitcast.144, ...), custom_call_target="tpu_custom_call", output_to_operand_aliasing={{}: (5, {})} | custom-call | flops 3623878656 | bytes 48000000 | tf_op jit(solution)/shard_map/forward/pallas_call | solution.py:183
  315.3 32.9 %collective-permute-done.16 = bf16[3,2,2,384,384]{4,3,2,1,0:T(8,128)(2,1)} collective-permute-done((bf16[3,2,2,384,384]{4,3,2,1,0:T(8,128)(2,1)S(1)}, bf16[3,2,2,384,384]{4,3,2,1,0:T(8,128)(2,1)}, u32[]{:S(2)}, u32[]{:S(2)}) %collective-permute-start.16) | collective-permute-done | bytes 3538976 | tf_op jit(solution)/shard_map/ppermute | solution.py:253
  348.7 10.8 %forward.5.mixed_ref = bf16[16,384,1024]{2,1,0:T(8,128)(2,1)} custom-call(s32[6]{0:T(128)} %stack.208.at_ref, s32[6]{0:T(128)} %iota.21.wat_ref, bf16[16,384,1024]{2,1,0:T(8,128)(2,1)} %spread.2.m_ref, bf16[6,2,384,384]{3,2,1,0:T(8,128)(2,1)} %bitcast.26.li_ref.ro_ref, ...), custom_call_target="tpu_custom_call", output_to_operand_aliasing={{}: (5, {})} | custom-call | flops 3623878656 | bytes 48000000 | tf_op jit(solution)/shard_map/forward/pallas_call | solution.py:183
  359.5 26.1 %gather.2 = (bf16[2,4,256,1536]{3,2,1,0:T(8,128)(2,1)}, bf16[2,4,256,1536]{3,2,1,0:T(8,128)(2,1)}, bf16[8,2,96,384]{3,2,1,0:T(8,128)(2,1)}) custom-call(s32[2]{0:T(128)} %pad_add_fusion.pos_ref, bf16[16,384,1024]{2,1,0:T(8,128)(2,1)} %forward.5.mixed_ref, bf16[4,256,1536]{2,1,0:T(8,128)(2,1)} %all-to-all-done.1.refs_0_, ...), custom_call_target="tpu_custom_call" | custom-call | flops 2415919104 | bytes 76000000 | tf_op jit(solution)/shard_map/gather/pallas_call | solution.py:149
  385.7 18.0 %spread.3.b_ref = bf16[16,384,1024]{2,1,0:T(8,128)(2,1)} custom-call(s32[2]{0:T(128)} %pad_add_fusion.pos_ref, bf16[4,256,1536]{2,1,0:T(8,128)(2,1)} %all-to-all-done.1.refs_0_, bf16[4,256,1536]{2,1,0:T(8,128)(2,1)} %collective-permute-done.17.refs_1_, bf16[4,256,1536]{2,1,0:T(8,128)(2,1)} %collective-permute-done.18.refs_2_, ...), custom_call_target="tpu_custom_call" | custom-call | flops 1207959552 | bytes 58000000 | tf_op jit(solution)/shard_map/spread/pallas_call | solution.py:70
  405.2 18.3 %backward.3 = (bf16[16,384,1024]{2,1,0:T(8,128)(2,1)}, bf16[6,2,4,96,384]{4,3,2,1,0:T(8,128)(2,1)}) custom-call(s32[6]{0:T(128)} %stack.233.at_ref, s32[6]{0:T(128)} %iota.25.wat_ref, bf16[16,384,1024]{2,1,0:T(8,128)(2,1)} %spread.2.m_ref, bf16[16,384,1024]{2,1,0:T(8,128)(2,1)} %spread.3.b_ref, ...), custom_call_target="tpu_custom_call", output_to_operand_aliasing={{0}: (3, {})} | custom-call | flops 9059696640 | bytes 90000000 | tf_op jit(solution)/shard_map/backward/pallas_call | solution.py:230
  439.6 18.1 %backward.4 = (bf16[16,384,1024]{2,1,0:T(8,128)(2,1)}, bf16[6,2,4,96,384]{4,3,2,1,0:T(8,128)(2,1)}) custom-call(s32[6]{0:T(128)} %stack.208.at_ref, s32[6]{0:T(128)} %iota.24.wat_ref, bf16[16,384,1024]{2,1,0:T(8,128)(2,1)} %spread.2.m_ref, bf16[16,384,1024]{2,1,0:T(8,128)(2,1)} %get-tuple-element.46.b_ref, ...), custom_call_target="tpu_custom_call", output_to_operand_aliasing={{0}: (3, {})} | custom-call | flops 9059696640 | bytes 90000000 | tf_op jit(solution)/shard_map/backward/pallas_call | solution.py:230
  457.7 6.9 collective-permute-done.21
  475.1 13.2 %backward.5 = (bf16[16,384,1024]{2,1,0:T(8,128)(2,1)}, bf16[4,2,4,96,384]{4,3,2,1,0:T(8,128)(2,1)}) custom-call(s32[4]{0:T(128)} %get-tuple-element.106.at_ref, s32[4]{0:T(128)} %get-tuple-element.107.wat_ref, bf16[16,384,1024]{2,1,0:T(8,128)(2,1)} %spread.2.m_ref, bf16[16,384,1024]{2,1,0:T(8,128)(2,1)} %get-tuple-element.50.b_ref, ...), custom_call_target="tpu_custom_call", output_to_operand_aliasing={{0}: (3, {})} | custom-call | flops 6039797760 | bytes 60000000 | tf_op jit(solution)/shard_map/backward/pallas_call | solution.py:230
  488.3 16.5 %collective-permute-done.24 = bf16[20,96,384]{2,1,0:T(8,128)(2,1)} collective-permute-done((bf16[20,96,384]{2,1,0:T(8,128)(2,1)}, bf16[20,96,384]{2,1,0:T(8,128)(2,1)}, u32[]{:S(2)}, u32[]{:S(2)}) %collective-permute-start.24) | collective-permute-done | bytes 1474592 | tf_op jit(solution)/shard_map/ppermute | solution.py:261
  508.1 26.1 %gather.3 = (bf16[2,4,256,1536]{3,2,1,0:T(8,128)(2,1)}, bf16[2,4,256,1536]{3,2,1,0:T(8,128)(2,1)}, bf16[8,2,96,384]{3,2,1,0:T(8,128)(2,1)}) custom-call(s32[2]{0:T(128)} %pad_add_fusion.pos_ref, bf16[16,384,1024]{2,1,0:T(8,128)(2,1)} %get-tuple-element.55.mixed_ref, bf16[4,256,1536]{2,1,0:T(8,128)(2,1)} %all-to-all-done.refs_0_, ...), custom_call_target="tpu_custom_call" | custom-call | flops 2415919104 | bytes 76000000 | tf_op jit(solution)/shard_map/gather/pallas_call | solution.py:149
  547.3 5.8 fusion.1
  562.5 13.5 %collective-permute-done.27 = bf16[20,96,384]{2,1,0:T(8,128)(2,1)} collective-permute-done((bf16[20,96,384]{2,1,0:T(8,128)(2,1)}, bf16[20,96,384]{2,1,0:T(8,128)(2,1)}, u32[]{:S(2)}, u32[]{:S(2)}) %collective-permute-start.27) | collective-permute-done | bytes 1474592 | tf_op jit(solution)/shard_map/ppermute | solution.py:261
  587.0 8.7 %collective-permute-start.36 = (bf16[20,96,384]{2,1,0:T(8,128)(2,1)}, bf16[20,96,384]{2,1,0:T(8,128)(2,1)}, u32[]{:S(2)}, u32[]{:S(2)}) collective-permute-start(bf16[20,96,384]{2,1,0:T(8,128)(2,1)} %add_convert_fusion.4), channel_id=1, source_target_pairs={{0,4},{4,8},{8,12},{1,5},{5,9},{9,13},{2,6},{6,10},{10,14},{3,7},{... | collective-permute-start | bytes 4423688 | tf_op jit(solution)/shard_map/ppermute | solution.py:261
  598.6 59.5 %collective-permute-done.28 = bf16[20,96,384]{2,1,0:T(8,128)(2,1)S(1)} collective-permute-done((bf16[20,96,384]{2,1,0:T(8,128)(2,1)S(1)}, bf16[20,96,384]{2,1,0:T(8,128)(2,1)S(1)}, u32[]{:S(2)}, u32[]{:S(2)}) %collective-permute-start.28) | collective-permute-done | bytes 1474592 | tf_op jit(solution)/shard_map/ppermute | solution.py:261
  659.7 6.2 collective-permute-start.32
  669.0 5.8 fusion
  674.8 7.0 all-to-all-start.3
  683.8 6.1 collective-permute-done.36
  695.4 26.1 %collective-permute-done.32 = bf16[20,96,384]{2,1,0:T(8,128)(2,1)} collective-permute-done((bf16[20,96,384]{2,1,0:T(8,128)(2,1)}, bf16[20,96,384]{2,1,0:T(8,128)(2,1)}, u32[]{:S(2)}, u32[]{:S(2)}) %collective-permute-start.32) | collective-permute-done | bytes 1474592 | tf_op jit(solution)/shard_map/ppermute | solution.py:261
  730.5 13.0 %collective-permute-done.34 = bf16[2,480,384]{2,1,0:T(8,128)(2,1)} collective-permute-done((bf16[2,480,384]{2,1,0:T(8,128)(2,1)}, bf16[2,480,384]{2,1,0:T(8,128)(2,1)}, u32[]{:S(2)}, u32[]{:S(2)}) %collective-permute-start.34) | collective-permute-done | bytes 737312 | tf_op jit(solution)/shard_map/ppermute | solution.py:253
  775.3 15.5 %all-to-all-done.3 = bf16[4,256,1536]{2,1,0:T(8,128)(2,1)} async-done(((bf16[4,256,1536]{2,1,0:T(8,128)(2,1)}), bf16[4,256,1536]{2,1,0:T(8,128)(2,1)}, u32[]{:S(2)}, u32[]{:S(2)}) %all-to-all-start.3) | async-done | bytes 3145760 | tf_op jit(solution)/shard_map/all_to_all | solution.py:276
  (223 shorter events, 193.3 us)
Async XLA Ops:
  0.6 113.5 %all-to-all-start = ((bf16[4,256,1536]{2,1,0:T(8,128)(2,1)}), bf16[4,256,1536]{2,1,0:T(8,128)(2,1)}, u32[]{:S(2)}, u32[]{:S(2)}) async-start(bf16[4,256,1536]{2,1,0:T(8,128)(2,1)} %bitcast.182), calls=%async_computation | async-start | bytes 6291456 | tf_op jit(solution)/shard_map/all_to_all | solution.py:276
  10.3 56.0 %collective-permute-start = (bf16[8,2,96,96]{2,3,1,0:T(8,128)(2,1)S(1)}, bf16[8,2,96,96]{2,3,1,0:T(8,128)(2,1)S(1)}, u32[]{:S(2)}, u32[]{:S(2)}) collective-permute-start(bf16[8,2,96,96]{2,3,1,0:T(8,128)(2,1)S(1)} %constant_dynamic-slice_fusion), channel_id=1, source_target_pairs={{0,4},{4,8},{8,12},{1,5},{5,9},{9,13},{2,6},{6,10},{10,14},{3,7},{... | collective-permute-start | bytes 884744 | tf_op jit(solution)/shard_map/ppermute | solution.py:261
  14.2 55.6 %collective-permute-start.3 = (bf16[8,2,96,96]{2,3,1,0:T(8,128)(2,1)S(1)}, bf16[8,2,96,96]{2,3,1,0:T(8,128)(2,1)}, u32[]{:S(2)}, u32[]{:S(2)}) collective-permute-start(bf16[8,2,96,96]{2,3,1,0:T(8,128)(2,1)S(1)} %constant_dynamic-slice_fusion), channel_id=1, source_target_pairs={{12,8},{8,4},{4,0},{13,9},{9,5},{5,1},{14,10},{10,6},{6,2},{15,11}... | collective-permute-start | bytes 884744 | tf_op jit(solution)/shard_map/ppermute | solution.py:265
  69.8 32.1 %collective-permute-start.4 = (bf16[8,2,96,96]{2,3,1,0:T(8,128)(2,1)}, bf16[8,2,96,96]{2,3,1,0:T(8,128)(2,1)}, u32[]{:S(2)}, u32[]{:S(2)}) collective-permute-start(bf16[8,2,96,96]{2,3,1,0:T(8,128)(2,1)} %collective-permute-done.3), channel_id=1, source_target_pairs={{8,4},{4,0},{9,5},{5,1},{10,6},{6,2},{11,7},{7,3},{24,20},{20,16},... | collective-permute-start | bytes 884744 | tf_op jit(solution)/shard_map/ppermute | solution.py:265
  73.4 30.9 %collective-permute-start.2 = (bf16[8,2,96,96]{2,3,1,0:T(8,128)(2,1)}, bf16[8,2,96,96]{2,3,1,0:T(8,128)(2,1)}, u32[]{:S(2)}, u32[]{:S(2)}) collective-permute-start(bf16[8,2,96,96]{2,3,1,0:T(8,128)(2,1)} %collective-permute-done.1), channel_id=1, source_target_pairs={{8,12},{9,13},{10,14},{11,15},{24,28},{25,29},{26,30},{27,31}} | collective-permute-start | bytes 884744 | tf_op jit(solution)/shard_map/ppermute | solution.py:261
  114.1 107.8 %all-to-all-start.1 = ((bf16[4,256,1536]{2,1,0:T(8,128)(2,1)}), bf16[4,256,1536]{2,1,0:T(8,128)(2,1)}, u32[]{:S(2)}, u32[]{:S(2)}) async-start(bf16[4,256,1536]{2,1,0:T(8,128)(2,1)} %bitcast.183), calls=%async_computation.1 | async-start | bytes 6291456 | tf_op jit(solution)/shard_map/all_to_all | solution.py:276
  118.8 80.1 %collective-permute-start.6 = (bf16[4,256,1536]{2,1,0:T(8,128)(2,1)}, bf16[4,256,1536]{2,1,0:T(8,128)(2,1)}, u32[]{:S(2)}, u32[]{:S(2)}) collective-permute-start(bf16[4,256,1536]{2,1,0:T(8,128)(2,1)} %all-to-all-done.refs_0_), channel_id=1, source_target_pairs={{0,2},{2,0},{1,3},{3,1},{4,6},{6,4},{5,7},{7,5},{8,10},{10,8},{9,1... | collective-permute-start | bytes 9437192 | tf_op jit(solution)/shard_map/ppermute | solution.py:253
  120.4 73.9 %collective-permute-start.13 = (bf16[2,2,384,384]{3,2,1,0:T(8,128)(2,1)}, bf16[2,2,384,384]{3,2,1,0:T(8,128)(2,1)}, u32[]{:S(2)}, u32[]{:S(2)}) collective-permute-start(bf16[2,2,384,384]{3,2,1,0:T(8,128)(2,1)} %fusion.10), channel_id=1, source_target_pairs={{12,8},{8,4},{4,0},{13,9},{9,5},{5,1},{14,10},{10,6},{6,2},{15,11}... | collective-permute-start | bytes 3538952 | tf_op jit(solution)/shard_map/ppermute | solution.py:265
  121.7 75.5 %collective-permute-start.10 = (bf16[2,2,384,384]{3,2,1,0:T(8,128)(2,1)}, bf16[2,2,384,384]{3,2,1,0:T(8,128)(2,1)}, u32[]{:S(2)}, u32[]{:S(2)}) collective-permute-start(bf16[2,2,384,384]{3,2,1,0:T(8,128)(2,1)} %fusion.10), channel_id=1, source_target_pairs={{0,4},{4,8},{8,12},{1,5},{5,9},{9,13},{2,6},{6,10},{10,14},{3,7},{... | collective-permute-start | bytes 3538952 | tf_op jit(solution)/shard_map/ppermute | solution.py:261
  194.3 45.7 %collective-permute-start.14 = (bf16[2,2,384,384]{3,2,1,0:T(8,128)(2,1)}, bf16[2,2,384,384]{3,2,1,0:T(8,128)(2,1)}, u32[]{:S(2)}, u32[]{:S(2)}) collective-permute-start(bf16[2,2,384,384]{3,2,1,0:T(8,128)(2,1)} %collective-permute-done.13), channel_id=1, source_target_pairs={{8,4},{4,0},{9,5},{5,1},{10,6},{6,2},{11,7},{7,3},{24,20},{20,16},... | collective-permute-start | bytes 3538952 | tf_op jit(solution)/shard_map/ppermute | solution.py:265
  197.2 44.1 %collective-permute-start.11 = (bf16[2,2,384,384]{3,2,1,0:T(8,128)(2,1)}, bf16[2,2,384,384]{3,2,1,0:T(8,128)(2,1)}, u32[]{:S(2)}, u32[]{:S(2)}) collective-permute-start(bf16[2,2,384,384]{3,2,1,0:T(8,128)(2,1)} %collective-permute-done.10), channel_id=1, source_target_pairs={{4,8},{8,12},{5,9},{9,13},{6,10},{10,14},{7,11},{11,15},{20,24},{2... | collective-permute-start | bytes 3538952 | tf_op jit(solution)/shard_map/ppermute | solution.py:261
  198.9 78.0 %collective-permute-start.7 = (bf16[4,256,1536]{2,1,0:T(8,128)(2,1)}, bf16[4,256,1536]{2,1,0:T(8,128)(2,1)}, u32[]{:S(2)}, u32[]{:S(2)}) collective-permute-start(bf16[4,256,1536]{2,1,0:T(8,128)(2,1)} %all-to-all-done.refs_0_), channel_id=1, source_target_pairs={{0,1},{1,0},{2,3},{3,2},{4,5},{5,4},{6,7},{7,6},{8,9},{9,8},{10,11... | collective-permute-start | bytes 9437192 | tf_op jit(solution)/shard_map/ppermute | solution.py:253
  198.9 78.0 %collective-permute-start.8 = (bf16[4,256,1536]{2,1,0:T(8,128)(2,1)}, bf16[4,256,1536]{2,1,0:T(8,128)(2,1)}, u32[]{:S(2)}, u32[]{:S(2)}) collective-permute-start(bf16[4,256,1536]{2,1,0:T(8,128)(2,1)} %collective-permute-done.6.refs_1_), channel_id=1, source_target_pairs={{0,1},{1,0},{2,3},{3,2},{4,5},{5,4},{6,7},{7,6},{8,9},{9,8},{10,11... | collective-permute-start | bytes 9437192 | tf_op jit(solution)/shard_map/ppermute | solution.py:253
  221.9 92.3 %collective-permute-start.17 = (bf16[4,256,1536]{2,1,0:T(8,128)(2,1)}, bf16[4,256,1536]{2,1,0:T(8,128)(2,1)}, u32[]{:S(2)}, u32[]{:S(2)}) collective-permute-start(bf16[4,256,1536]{2,1,0:T(8,128)(2,1)} %all-to-all-done.1.refs_0_), channel_id=1, source_target_pairs={{0,2},{2,0},{1,3},{3,1},{4,6},{6,4},{5,7},{7,5},{8,10},{10,8},{9,1... | collective-permute-start | bytes 9437192 | tf_op jit(solution)/shard_map/ppermute | solution.py:253
  272.4 75.8 %collective-permute-start.16 = (bf16[3,2,2,384,384]{4,3,2,1,0:T(8,128)(2,1)S(1)}, bf16[3,2,2,384,384]{4,3,2,1,0:T(8,128)(2,1)}, u32[]{:S(2)}, u32[]{:S(2)}) collective-permute-start(bf16[3,2,2,384,384]{4,3,2,1,0:T(8,128)(2,1)S(1)} %pad_maximum_fusion), channel_id=1, source_target_pairs={{0,16},{16,0},{1,17},{17,1},{2,18},{18,2},{3,19},{19,3},{4,20},{20... | collective-permute-start | bytes 10616840 | tf_op jit(solution)/shard_map/ppermute | solution.py:253
  276.9 82.6 %collective-permute-start.18 = (bf16[4,256,1536]{2,1,0:T(8,128)(2,1)}, bf16[4,256,1536]{2,1,0:T(8,128)(2,1)}, u32[]{:S(2)}, u32[]{:S(2)}) collective-permute-start(bf16[4,256,1536]{2,1,0:T(8,128)(2,1)} %all-to-all-done.1.refs_0_), channel_id=1, source_target_pairs={{0,1},{1,0},{2,3},{3,2},{4,5},{5,4},{6,7},{7,6},{8,9},{9,8},{10,11... | collective-permute-start | bytes 9437192 | tf_op jit(solution)/shard_map/ppermute | solution.py:253
  314.2 45.3 %collective-permute-start.19 = (bf16[4,256,1536]{2,1,0:T(8,128)(2,1)}, bf16[4,256,1536]{2,1,0:T(8,128)(2,1)}, u32[]{:S(2)}, u32[]{:S(2)}) collective-permute-start(bf16[4,256,1536]{2,1,0:T(8,128)(2,1)} %collective-permute-done.17.refs_1_), channel_id=1, source_target_pairs={{0,1},{1,0},{2,3},{3,2},{4,5},{5,4},{6,7},{7,6},{8,9},{9,8},{10,11... | collective-permute-start | bytes 9437192 | tf_op jit(solution)/shard_map/ppermute | solution.py:253
  430.6 33.9 %collective-permute-start.21 = (bf16[20,96,384]{2,1,0:T(8,128)(2,1)}, bf16[20,96,384]{2,1,0:T(8,128)(2,1)}, u32[]{:S(2)}, u32[]{:S(2)}) collective-permute-start(bf16[20,96,384]{2,1,0:T(8,128)(2,1)} %pad_maximum_fusion.3), channel_id=1, source_target_pairs={{0,4},{1,5},{2,6},{3,7},{16,20},{17,21},{18,22},{19,23}} | collective-permute-start | bytes 4423688 | tf_op jit(solution)/shard_map/ppermute | solution.py:261
  437.7 70.4 %collective-permute-start.23 = (bf16[4,256,1536]{2,1,0:T(8,128)(2,1)}, bf16[4,256,1536]{2,1,0:T(8,128)(2,1)}, u32[]{:S(2)}, u32[]{:S(2)}) collective-permute-start(bf16[4,256,1536]{2,1,0:T(8,128)(2,1)} %fusion.2), channel_id=1, source_target_pairs={{0,2},{2,0},{1,3},{3,1},{4,6},{6,4},{5,7},{7,5},{8,10},{10,8},{9,1... | collective-permute-start | bytes 9437192 | tf_op jit(solution)/shard_map/ppermute | solution.py:253
  468.7 36.0 %collective-permute-start.24 = (bf16[20,96,384]{2,1,0:T(8,128)(2,1)}, bf16[20,96,384]{2,1,0:T(8,128)(2,1)}, u32[]{:S(2)}, u32[]{:S(2)}) collective-permute-start(bf16[20,96,384]{2,1,0:T(8,128)(2,1)} %get-tuple-element.97), channel_id=1, source_target_pairs={{0,4},{4,8},{1,5},{5,9},{2,6},{6,10},{3,7},{7,11},{16,20},{20,24},... | collective-permute-start | bytes 4423688 | tf_op jit(solution)/shard_map/ppermute | solution.py:261
  540.3 35.8 %collective-permute-start.27 = (bf16[20,96,384]{2,1,0:T(8,128)(2,1)}, bf16[20,96,384]{2,1,0:T(8,128)(2,1)}, u32[]{:S(2)}, u32[]{:S(2)}) collective-permute-start(bf16[20,96,384]{2,1,0:T(8,128)(2,1)} %pad_maximum_fusion.7), channel_id=1, source_target_pairs={{0,4},{1,5},{2,6},{3,7},{16,20},{17,21},{18,22},{19,23}} | collective-permute-start | bytes 4423688 | tf_op jit(solution)/shard_map/ppermute | solution.py:261
  545.5 30.5 %collective-permute-start.29 = (bf16[20,96,384]{2,1,0:T(8,128)(2,1)}, bf16[20,96,384]{2,1,0:T(8,128)(2,1)}, u32[]{:S(2)}, u32[]{:S(2)}) collective-permute-start(bf16[20,96,384]{2,1,0:T(8,128)(2,1)} %pad_maximum_fusion.8), channel_id=1, source_target_pairs={{12,8},{13,9},{14,10},{15,11},{28,24},{29,25},{30,26},{31,27}} | collective-permute-start | bytes 4423688 | tf_op jit(solution)/shard_map/ppermute | solution.py:265
  553.1 121.7 %all-to-all-start.2 = ((bf16[4,256,1536]{2,1,0:T(8,128)(2,1)}), bf16[4,256,1536]{2,1,0:T(8,128)(2,1)S(1)}, u32[]{:S(2)}, u32[]{:S(2)}) async-start(bf16[4,256,1536]{2,1,0:T(8,128)(2,1)} %fusion.1), calls=%async_computation.2 | async-start | bytes 6291456 | tf_op jit(solution)/shard_map/all_to_all | solution.py:276
  561.0 97.2 %collective-permute-start.31 = (bf16[4,256,1536]{2,1,0:T(8,128)(2,1)S(1)}, bf16[4,256,1536]{2,1,0:T(8,128)(2,1)S(1)}, u32[]{:S(2)}, u32[]{:S(2)}) collective-permute-start(bf16[4,256,1536]{2,1,0:T(8,128)(2,1)S(1)} %fusion.3), channel_id=1, source_target_pairs={{0,2},{2,0},{1,3},{3,1},{4,6},{6,4},{5,7},{7,5},{8,10},{10,8},{9,1... | collective-permute-start | bytes 9437192 | tf_op jit(solution)/shard_map/ppermute | solution.py:253
  578.7 79.5 %collective-permute-start.28 = (bf16[20,96,384]{2,1,0:T(8,128)(2,1)S(1)}, bf16[20,96,384]{2,1,0:T(8,128)(2,1)S(1)}, u32[]{:S(2)}, u32[]{:S(2)}) collective-permute-start(bf16[20,96,384]{2,1,0:T(8,128)(2,1)S(1)} %get-tuple-element.95), channel_id=1, source_target_pairs={{0,4},{4,8},{1,5},{5,9},{2,6},{6,10},{3,7},{7,11},{16,20},{20,24},... | collective-permute-start | bytes 4423688 | tf_op jit(solution)/shard_map/ppermute | solution.py:261
  583.2 75.0 %collective-permute-start.30 = (bf16[20,96,384]{2,1,0:T(8,128)(2,1)S(1)}, bf16[20,96,384]{2,1,0:T(8,128)(2,1)S(1)}, u32[]{:S(2)}, u32[]{:S(2)}) collective-permute-start(bf16[20,96,384]{2,1,0:T(8,128)(2,1)S(1)} %get-tuple-element.94), channel_id=1, source_target_pairs={{12,8},{8,4},{13,9},{9,5},{14,10},{10,6},{15,11},{11,7},{28,24},{2... | collective-permute-start | bytes 4423688 | tf_op jit(solution)/shard_map/ppermute | solution.py:265
  587.0 102.9 %collective-permute-start.36 = (bf16[20,96,384]{2,1,0:T(8,128)(2,1)}, bf16[20,96,384]{2,1,0:T(8,128)(2,1)}, u32[]{:S(2)}, u32[]{:S(2)}) collective-permute-start(bf16[20,96,384]{2,1,0:T(8,128)(2,1)} %add_convert_fusion.4), channel_id=1, source_target_pairs={{0,4},{4,8},{8,12},{1,5},{5,9},{9,13},{2,6},{6,10},{10,14},{3,7},{... | collective-permute-start | bytes 4423688 | tf_op jit(solution)/shard_map/ppermute | solution.py:261
  597.2 92.7 %collective-permute-start.37 = (bf16[20,96,384]{2,1,0:T(8,128)(2,1)}, bf16[20,96,384]{2,1,0:T(8,128)(2,1)}, u32[]{:S(2)}, u32[]{:S(2)}) collective-permute-start(bf16[20,96,384]{2,1,0:T(8,128)(2,1)} %add_convert_fusion.3), channel_id=1, source_target_pairs={{12,8},{8,4},{4,0},{13,9},{9,5},{5,1},{14,10},{10,6},{6,2},{15,11}... | collective-permute-start | bytes 4423688 | tf_op jit(solution)/shard_map/ppermute | solution.py:265
  659.7 61.8 %collective-permute-start.32 = (bf16[20,96,384]{2,1,0:T(8,128)(2,1)}, bf16[20,96,384]{2,1,0:T(8,128)(2,1)}, u32[]{:S(2)}, u32[]{:S(2)}) collective-permute-start(bf16[20,96,384]{2,1,0:T(8,128)(2,1)} %add_convert_fusion.7), channel_id=1, source_target_pairs={{0,4},{4,8},{8,12},{1,5},{5,9},{9,13},{2,6},{6,10},{10,14},{3,7},{... | collective-permute-start | bytes 4423688 | tf_op jit(solution)/shard_map/ppermute | solution.py:261
  667.5 54.0 %collective-permute-start.33 = (bf16[20,96,384]{2,1,0:T(8,128)(2,1)}, bf16[20,96,384]{2,1,0:T(8,128)(2,1)}, u32[]{:S(2)}, u32[]{:S(2)}) collective-permute-start(bf16[20,96,384]{2,1,0:T(8,128)(2,1)} %add_convert_fusion.6), channel_id=1, source_target_pairs={{12,8},{8,4},{4,0},{13,9},{9,5},{5,1},{14,10},{10,6},{6,2},{15,11}... | collective-permute-start | bytes 4423688 | tf_op jit(solution)/shard_map/ppermute | solution.py:265
  674.8 116.0 %all-to-all-start.3 = ((bf16[4,256,1536]{2,1,0:T(8,128)(2,1)}), bf16[4,256,1536]{2,1,0:T(8,128)(2,1)}, u32[]{:S(2)}, u32[]{:S(2)}) async-start(bf16[4,256,1536]{2,1,0:T(8,128)(2,1)} %fusion), calls=%async_computation.3 | async-start | bytes 6291456 | tf_op jit(solution)/shard_map/all_to_all | solution.py:276
  693.9 33.1 %collective-permute-start.38 = (bf16[2,480,384]{2,1,0:T(8,128)(2,1)}, bf16[2,480,384]{2,1,0:T(8,128)(2,1)}, u32[]{:S(2)}, u32[]{:S(2)}) collective-permute-start(bf16[2,480,384]{2,1,0:T(8,128)(2,1)} %get-tuple-element.89), channel_id=1, source_target_pairs={{0,2},{2,0},{1,3},{3,1},{4,6},{6,4},{5,7},{7,5},{8,10},{10,8},{9,1... | collective-permute-start | bytes 2211848 | tf_op jit(solution)/shard_map/ppermute | solution.py:253
  (48 other events, 917.6 us)

commit v2 on v1

--- a/solution.py
+++ b/solution.py
@@ -144,6 +144,10 @@
         t, k = place(i, pos)
         return 0, t, 0, k
 
+    def grad_map(i, pos):
+        t, k = place(i, pos)
+        return t * per + k, 0, 0, 0
+
     act = pl.BlockSpec((1, count, PACK * wide), act_map)
     out = pl.BlockSpec((half, 1, count, PACK * wide), out_map)
     return pl.pallas_call(
@@ -154,7 +158,7 @@
             in_specs=[pl.BlockSpec((TAIL, blocks * part, lanes), lambda i, pos: (jnp.minimum(i, lead - 1), 0, 0))]
             + [act] * len(acts)
             + [pl.BlockSpec((PACK, 1, wide, rows), lambda i, pos: (jnp.maximum(i - lead, 0), which, 0, 0))],
-            out_specs=[out, out, pl.BlockSpec((1, 2, rows, PACK // 2 * wide), lambda i, pos: (jnp.maximum(i - lead, 0), 0, 0, 0))],
+            out_specs=[out, out, pl.BlockSpec((1, 2, rows, PACK // 2 * wide), grad_map)],
             scratch_shapes=[scratch(blocks, rows, lanes)],
         ),
         out_shape=[jax.ShapeDtypeStruct((half, quarters, count, span), BF16)] * 2
@@ -293,11 +297,13 @@
     place = jnp.arange(hid)
     reorder = (place[:, None] % blocks * part + place[:, None] // blocks == place[None, :]).astype(BF16)
 
+    def selected(u1, d1, u2, d2, u3, d3):
+        return jnp.stack([jnp.where(z == 3, u3, d1), jnp.where(z < 2, d2, u2), jnp.where(z == 0, d3, u1)])
+
     def line_gather(a):
         u1, d1 = up(a, 0, 3), down(a, 3, 0)
         u2, d2 = up(u1, 1, 3), down(d1, 2, 0)
-        u3, d3 = up(u2, 2, 3), down(d2, 1, 0)
-        return jnp.stack([jnp.where(z == 3, u3, d1), jnp.where(z < 2, d2, u2), jnp.where(z == 0, d3, u1)])
+        return u1, d1, u2, d2, up(u2, 2, 3), down(d2, 1, 0)
 
     def by_group(a, b):
         return jnp.where(g == 0, jnp.stack([a, b], axis=1), jnp.stack([b, a], axis=1))
@@ -305,7 +311,7 @@
     small = jnp.stack([right_in, jnp.swapaxes(left_out, 1, 2)], axis=1)
     small = small.reshape(nb, 2, wide, 4, 4, own_nb * part)
     small = lax.dynamic_index_in_dim(small, mate, axis=4, keepdims=False).reshape(nb, 2, wide, hid // 4)
-    fs = line_gather(lax.dynamic_slice_in_dim(small, g * (nb // 2), nb // 2, axis=0))
+    fs = selected(*line_gather(lax.dynamic_slice_in_dim(small, g * (nb // 2), nb // 2, axis=0)))
 
     own_li = lax.dynamic_slice_in_dim(left_in, mate * own_nb, own_nb, axis=0)
     own_ro = lax.dynamic_slice_in_dim(right_out, mate * own_nb, own_nb, axis=0)
@@ -315,96 +321,106 @@
 
     own_x = all_to_all(tokens.reshape(4, rows // 4, span))
     x_x = swap(own_x, "x")
-    cotangent, mine, own_x, fs = lax.optimization_barrier((cotangent, lax.dynamic_slice_in_dim(own_w, 2 * g, 2, axis=0), own_x, fs))
+    cotangent, own_x, fs, own_w = lax.optimization_barrier((cotangent, own_x, fs, own_w))
     own_y = all_to_all(cotangent.reshape(4, rows // 4, span))
     acts_x = [own_x, x_x, swap(own_x, "core"), swap(x_x, "core")]
-    f = line_gather(mine)
-    yf = swap(f, "groups")
+    mine = lax.dynamic_slice_in_dim(own_w, 2 * g, 2, axis=0)
+    u1, d1 = up(mine, 0, 3), down(mine, 3, 0)
+    own_y, ys, u1, d1 = lax.optimization_barrier((own_y, swap(fs, "groups"), u1, d1))
+    u2, d2 = up(u1, 1, 3), down(d1, 2, 0)
+    small = jnp.concatenate([small, by_group(fs, ys).reshape(3 * nb, *small.shape[1:])])
+    mixed = spread(pos, acts_x, small, 0, part)
     x_y = swap(own_y, "x")
-    small = jnp.concatenate([small, by_group(fs, swap(fs, "groups")).reshape(3 * nb, *small.shape[1:])])
-
+    u2, d2, mixed = lax.optimization_barrier((u2, d2, mixed))
+    hops = u1, d1, u2, d2, up(u2, 2, 3), down(d2, 1, 0)
     order = [(gr, h) for gr in range(2) for h in range(2)]
     index = {(gr, h): 2 * ((g + gr) % 2) + h for gr, h in order}
     six = jnp.arange(6, dtype=jnp.int32)
-    pieces = [
-        (jnp.stack([z * own_nb + index[o] for o in order]).astype(jnp.int32), jnp.stack([index[o] for o in order]).astype(jnp.int32), own_w)
-    ]
+    own_at = jnp.stack([z * own_nb + index[o] for o in order]).astype(jnp.int32)
+    own_wat = jnp.stack([index[o] for o in order]).astype(jnp.int32)
+    second = forward(own_at, own_wat, mixed, own_w, None)
+    x_y, second, *hops = lax.optimization_barrier((x_y, second, *hops))
+    acts_y = [own_y, x_y, swap(own_y, "core"), swap(x_y, "core")]
+    f, x_y = lax.optimization_barrier((selected(*hops), x_y))
+    yf = swap(f, "groups")
+    back = spread(pos, acts_y, small, 1, part)
+    pieces = [(own_at, own_wat, own_w)]
     for gr, w in enumerate((f, yf)):
         at = [(z + r) % 4 * own_nb + index[gr, h] for r in (1, 2, 3) for h in range(2)]
         pieces.append((jnp.stack(at).astype(jnp.int32), six, w.reshape(6, 2, hid, hid)))
 
-    mixed = spread(pos, acts_x, small, 0, part)
-    second = None
-    for at, wat, w in pieces:
-        if w is pieces[2][2]:
-            second, x_y = lax.optimization_barrier((second, x_y))
-        second = forward(at, wat, mixed, w, second)
-    acts_y = [own_y, x_y, swap(own_y, "core"), swap(x_y, "core")]
-    keep, send, lo = gather(pos, second, acts_y, small, 1, part)
-    got = swap(send, "core")
-    back = spread(pos, acts_y, small, 1, part)
-    back, got = lax.optimization_barrier((back, got))
-    out_x = swap(add(keep[1], got[1]).astype(BF16), "x")
-    out = add(keep[0], got[0])
-
-    grads = {}
-
     def step(n):
         at, wat, w = pieces[n]
         return backward(at, wat, mixed, back, w, blocks)
 
-    def shares(n, first):
-        first = first.reshape(4, -1, hid // 4, hid)
-        by_place = grads[n].reshape(3, -1, hid // 4, hid)
-        return [jnp.concatenate([by_place[r], first[r + 1]]) for r in range(3)]
-
-    def first_hop(s):
-        return up(s[2], 0, 1), down(s[0], 3, 2)
-
-    def second_hop(s, u, d):
-        return up(add(s[1], u).astype(BF16), 0, 2), down(add(s[1], d).astype(BF16), 3, 1)
-
-    def third_hop(s, u, d):
-        return up(add(s[0], u).astype(BF16), 0, 3), down(add(s[2], d).astype(BF16), 3, 0)
-
+    def step_forward(n):
+        at, wat, w = pieces[n]
+        return forward(at, wat, mixed, w, second)
+
+    def line(n):
+        return grads[n].reshape(3, -1, hid // 4, hid)
+
+    def plus(a, u, d):
+        return add(a, u).astype(BF16), add(a, d).astype(BF16)
+
+    def plus_two(a, u, b, d):
+        return add(a, u).astype(BF16), add(b, d).astype(BF16)
+
+    hold = lax.optimization_barrier
+    grads = {}
     back, grads[1] = step(1)
-    s1 = shares(1, lo)
-    u, d = first_hop(s1)
+    s1 = line(1)
+    u, d = up(s1[2], 0, 1), down(s1[0], 3, 2)
+    back, second = hold((back, second))
+    second = step_forward(1)
+    back, second = hold((back, second))
+    back, grads[0] = step(0)
+    back, u, d = hold((back, u, d))
+    back, u, d = hold((back, *plus(s1[1], u, d)))
+    u, d = up(u, 0, 2), down(d, 3, 1)
     back, grads[2] = step(2)
-    back, u, d = lax.optimization_barrier((back, u, d))
-    u, d = second_hop(s1, u, d)
-    back, grads[0] = step(0)
-    back, out_x, u, d = lax.optimization_barrier((back, out_x, u, d))
-    output = all_to_all(add(out, out_x).astype(BF16)).reshape(rows, span)
-    u1, d1 = third_hop(s1, u, d)
+    s2 = line(2)
+    v, e = up(s2[2], 0, 1), down(s2[0], 3, 2)
+    back, u, d = hold((back, u, d))
+    back, u, d = hold((back, *plus_two(s1[0], u, s1[2], d)))
+    u1, d1 = up(u, 0, 3), down(d, 3, 0)
     keep, send, ri = gather(pos, back, acts_x, small, 0, part)
+    second, keep, send, v, e = hold((second, keep, send, v, e))
     got = swap(send, "core")
-    gx_x = swap(add(keep[1], got[1]).astype(BF16), "x")
-    s2 = shares(2, ri)
-    u, d = first_hop(s2)
-    u, d = second_hop(s2, u, d)
-    u, d, gx_x = lax.optimization_barrier((u, d, gx_x))
-    grad_tokens = all_to_all(add(add(keep[0], got[0]), gx_x).astype(BF16)).reshape(rows, span)
-    v1, e1 = third_hop(s2, u, d)
-
-    def reduced(n, first, u1, d1):
-        own = grads[0].reshape(2, -1, hid // 4, hid)[n - 1]
-        count = own.shape[0]
-        total = add(jnp.concatenate([own, first.reshape(4, -1, hid // 4, hid)[0]]), u1, d1).astype(BF16)
-        second = total[:count].reshape(-1, 2, 2, hid // 4, hid).transpose(1, 2, 0, 3, 4).reshape(2, 2, -1, hid)
-        first = total[count:].reshape(-1, 2, 2, hid // 16, hid).transpose(1, 2, 0, 3, 4).reshape(2, 2, -1, hid)
-        total = jnp.concatenate([second, first], axis=2)
+    ri = lax.psum_scatter(ri.reshape(4, -1, hid // 4, hid), "tensor", scatter_dimension=0)
+    second, v, e = hold((second, *plus(s2[1], v, e)))
+    v, e = up(v, 0, 2), down(e, 3, 1)
+    second = step_forward(2)
+    second, got, u1, d1 = hold((second, got, u1, d1))
+    second, gx_x = hold((second, add(keep[1], got[1]).astype(BF16)))
+    gx_x = swap(gx_x, "x")
+    gx = add(keep[0], got[0])
+    keep, send, lo = gather(pos, second, acts_y, small, 1, part)
+    send, v, e = hold((send, v, e))
+    v, e = plus_two(s2[0], v, s2[2], e)
+    v1, e1 = up(v, 0, 3), down(e, 3, 0)
+    gx_x, send, v1, e1, ri = hold((gx_x, send, v1, e1, ri))
+    gx = add(gx, gx_x).astype(BF16)
+    grad_tokens = all_to_all(gx).reshape(rows, span)
+    got = swap(send, "core")
+    lo = lax.psum_scatter(lo.reshape(4, -1, hid // 4, hid), "tensor", scatter_dimension=0)
+    out_x = swap(add(keep[1], got[1]).astype(BF16), "x")
+    output = all_to_all(add(add(keep[0], got[0]), out_x).astype(BF16)).reshape(rows, span)
+
+    def split(total):
+        total = total.reshape(-1, 2, 2, total.shape[1] // 4, hid).transpose(1, 2, 0, 3, 4).reshape(2, 2, -1, hid)
         kept = lax.dynamic_index_in_dim(total, x, axis=0, keepdims=False)
         got = swap(lax.dynamic_index_in_dim(total, 1 - x, axis=0, keepdims=False), "x")
         total = jnp.where(x == 0, jnp.stack([kept, got], axis=1), jnp.stack([got, kept], axis=1))
         kept = lax.dynamic_index_in_dim(total, core, axis=0, keepdims=False)
         got = swap(lax.dynamic_index_in_dim(total, 1 - core, axis=0, keepdims=False), "core")
-        total = jnp.where(core == 0, jnp.stack([kept, got], axis=1), jnp.stack([got, kept], axis=1)).reshape(4, -1, hid)
-        cut = second.shape[2]
-        return total[:, :cut].reshape(4, 2, 2, hid // 4, hid), total[:, cut:].reshape(4, nb // PACK, 2, hid // 16, PACK // 2, wide)
-
-    big0, grad_lo = reduced(1, lo, u1, d1)
-    big1, grad_ri = reduced(2, ri, v1, e1)
+        return jnp.where(core == 0, jnp.stack([kept, got], axis=1), jnp.stack([got, kept], axis=1)).reshape(4, -1, hid)
+
+    own = grads[0].reshape(2, -1, hid // 4, hid)
+    big0 = split(add(own[0], u1, d1).astype(BF16).reshape(-1, hid, hid)).reshape(4, 2, 2, hid // 4, hid)
+    big1 = split(add(own[1], v1, e1).astype(BF16).reshape(-1, hid, hid)).reshape(4, 2, 2, hid // 4, hid)
+    first = split(jnp.concatenate([lo, ri])).reshape(4, 2, nb // PACK, 2, hid // 16, PACK // 2, wide)
+    grad_lo, grad_ri = first[:, 0], first[:, 1]
     big = by_group(big0, big1).reshape(nb, 2, hid // 4, hid)
     grad_li = jnp.einsum("cmp,pk->cmk", big[:, 0], reorder, preferred_element_type=F32) * scale
     grad_li = jnp.swapaxes(grad_li, 1, 2)

time: 805 us -> 766 us (0.952)
  waiting for transfers between devices: 398 us -> 362 us
  between operations: 1.74 us -> 14.9 us
  starting transfers between devices: 98.9 us -> 90.3 us
    ppermute x16 -> x18, waiting for transfers between devices: 71.8 us -> 191 us  [swap(): return lax.ppermute(a, axis, [(0, 1), (1, 0)])]
    ppermute x12, waiting for transfers between devices: 179 us -> 77.5 us  [up(): return lax.ppermute(a, 'tensor', [(i, i + 1) for i in range(first, last)])]
    ppermute x12, waiting for transfers between devices: 131 us -> 83.1 us  [down(): lax.ppermute(a, 'tensor', [(i, i - 1) for i in range(first, last, -1)])]
  transfers between devices with their start and end apart: 44 -> 48, of which waited for: 17 -> 17; matrix products, arithmetic and copies ran while one was open for 15% -> 15% of each run, Pallas kernels for 12% -> 22%
where the time goes in v2:
time: 766 us; the launch traced here: 756 us
  waiting for transfers between devices  362 us (47%)
  Pallas kernels  168 us (22%)
  starting transfers between devices  90.3 us (12%)
  other arithmetic  71.1 us (9%)
  local copies, waits for them, and re-layouts  43.4 us (6%)
  between operations  14.9 us (2%)
    ppermute x18, waiting for transfers between devices, swap(): return lax.ppermute(a, axis, [(0, 1), (1, 0)])  191 us
    ppermute x12, waiting for transfers between devices, down(): lax.ppermute(a, 'tensor', [(i, i - 1) for i in range(first, last, -1)])  83.1 us
    ppermute x12, waiting for transfers between devices, up(): return lax.ppermute(a, 'tensor', [(i, i + 1) for i in range(first, last)])  77.5 us
    pallas_call x2, Pallas kernels, gather(): pl.pallas_call(functools.partial(gather_kernel, lead, blocks, part), grid...  52.8 us
    pallas_call x3, Pallas kernels, backward(): pl.pallas_call(functools.partial(backward_kernel, blocks), grid_spec=pltp...  49 us
    ppermute x12, starting transfers between devices, up(): return lax.ppermute(a, 'tensor', [(i, i + 1) for i in range(first, last)])  42.3 us
    pallas_call x2, Pallas kernels, spread(): pl.pallas_call(functools.partial(spread_kernel, steps, blocks, part), gri...  35.9 us
    pallas_call x3, Pallas kernels, forward(): pl.pallas_call(forward_kernel, grid_spec=pltpu.PrefetchScalarGridSpec(num...  29.8 us
  transfers between devices with their start and end apart: 48, of which 17 were waited for; matrix products, arithmetic and copies ran while one was open for 15% of the time, Pallas kernels for 22%

profile of v2, /device:TPU:0, one launch (start us, length us, event | category | flops | bytes accessed | tf_op | source)
XLA Modules:
  0.0 756.2 jit_solution(5451407616044825125)
XLA Ops:
  7.2 6.5 all-to-all-start
  22.1 50.8 %collective-permute-done = bf16[8,2,96,96]{2,3,1,0:T(8,128)(2,1)S(1)} collective-permute-done((bf16[8,2,96,96]{2,3,1,0:T(8,128)(2,1)S(1)}, bf16[8,2,96,96]{2,3,1,0:T(8,128)(2,1)S(1)}, u32[]{:S(2)}, u32[]{:S(2)}) %collective-permute-start) | collective-permute-done | bytes 294944 | tf_op jit(solution)/shard_map/ppermute | solution.py:265
  81.6 26.8 %collective-permute-done.4 = bf16[8,2,96,96]{2,3,1,0:T(8,128)(2,1)} collective-permute-done((bf16[8,2,96,96]{2,3,1,0:T(8,128)(2,1)}, bf16[8,2,96,96]{2,3,1,0:T(8,128)(2,1)}, u32[]{:S(2)}, u32[]{:S(2)}) %collective-permute-start.4) | collective-permute-done | bytes 294944 | tf_op jit(solution)/shard_map/ppermute | solution.py:269
  111.9 7.4 collective-permute-done.5
  126.9 65.6 %collective-permute-done.11.refs_1_ = bf16[4,256,1536]{2,1,0:T(8,128)(2,1)} collective-permute-done((bf16[4,256,1536]{2,1,0:T(8,128)(2,1)}, bf16[4,256,1536]{2,1,0:T(8,128)(2,1)}, u32[]{:S(2)}, u32[]{:S(2)}) %collective-permute-start.11) | collective-permute-done | bytes 3145760 | tf_op jit(solution)/shard_map/ppermute | solution.py:257
  199.3 26.6 %collective-permute-done.6 = bf16[3,8,2,96,96]{3,4,2,1,0:T(8,128)(2,1)S(1)} collective-permute-done((bf16[3,8,2,96,96]{3,4,2,1,0:T(8,128)(2,1)S(1)}, bf16[3,8,2,96,96]{3,4,2,1,0:T(8,128)(2,1)S(1)}, u32[]{:S(2)}, u32[]{:S(2)}) %collective-permute-start.6) | collective-permute-done | bytes 884768 | tf_op jit(solution)/shard_map/ppermute | solution.py:257
  240.8 18.0 %spread.2.m_ref = bf16[16,384,1024]{2,1,0:T(8,128)(2,1)} custom-call(s32[2]{0:T(128)} %pad_add_fusion.pos_ref, bf16[4,256,1536]{2,1,0:T(8,128)(2,1)} %all-to-all-done.refs_0_, bf16[4,256,1536]{2,1,0:T(8,128)(2,1)} %collective-permute-done.11.refs_1_, bf16[4,256,1536]{2,1,0:T(8,128)(2,1)} %collective-permute-done.12.refs_2_, ...), custom_call_target="tpu_custom_call" | custom-call | flops 1207959552 | bytes 58000000 | tf_op jit(solution)/shard_map/spread/pallas_call | solution.py:70
  261.7 8.0 %forward.3.refs_0_ = bf16[16,384,1024]{2,1,0:T(8,128)(2,1)} custom-call(s32[4]{0:T(128)} %get-tuple-element.184.at_ref, s32[4]{0:T(128)} %get-tuple-element.185.wat_ref, bf16[16,384,1024]{2,1,0:T(8,128)(2,1)} %spread.2.m_ref, bf16[4,2,384,384]{3,2,1,0:T(8,128)(2,1)} %copy-done, bf16[4,2,384,384]{3,2,1,0:T(8,128)(2,1)} %copy-done), custom_call_target="tpu_custom_call" | custom-call | flops 2415919104 | bytes 32000000 | tf_op jit(solution)/shard_map/forward/pallas_call | solution.py:187
  269.7 23.0 %collective-permute-done.16 = bf16[2,2,384,384]{3,2,1,0:T(8,128)(2,1)S(1)} collective-permute-done((bf16[2,2,384,384]{3,2,1,0:T(8,128)(2,1)}, bf16[2,2,384,384]{3,2,1,0:T(8,128)(2,1)S(1)}, u32[]{:S(2)}, u32[]{:S(2)}) %collective-permute-start.16) | collective-permute-done | bytes 1179680 | tf_op jit(solution)/shard_map/ppermute | solution.py:269
  302.8 17.9 %spread.3.b_ref = bf16[16,384,1024]{2,1,0:T(8,128)(2,1)} custom-call(s32[2]{0:T(128)} %pad_add_fusion.pos_ref, bf16[4,256,1536]{2,1,0:T(8,128)(2,1)} %all-to-all-done.1.refs_0_, bf16[4,256,1536]{2,1,0:T(8,128)(2,1)} %collective-permute-done.14.refs_1_, bf16[4,256,1536]{2,1,0:T(8,128)(2,1)} %collective-permute-done.18.refs_2_, ...), custom_call_target="tpu_custom_call" | custom-call | flops 1207959552 | bytes 58000000 | tf_op jit(solution)/shard_map/spread/pallas_call | solution.py:70
  321.2 18.0 %backward.3 = (bf16[16,384,1024]{2,1,0:T(8,128)(2,1)}, bf16[6,2,4,96,384]{4,3,2,1,0:T(8,128)(2,1)}) custom-call(s32[6]{0:T(128)} %stack.271.at_ref, s32[6]{0:T(128)} %iota.23.wat_ref, bf16[16,384,1024]{2,1,0:T(8,128)(2,1)} %spread.2.m_ref, bf16[16,384,1024]{2,1,0:T(8,128)(2,1)} %spread.3.b_ref, ...), custom_call_target="tpu_custom_call", output_to_operand_aliasing={{0}: (3, {})} | custom-call | flops 9059696640 | bytes 90000000 | tf_op jit(solution)/shard_map/backward/pallas_call | solution.py:234
  343.0 5.0 collective-permute-start.20
  350.8 10.8 %forward.4.refs_0_ = bf16[16,384,1024]{2,1,0:T(8,128)(2,1)} custom-call(s32[6]{0:T(128)} %stack.271.at_ref, s32[6]{0:T(128)} %iota.24.wat_ref, bf16[16,384,1024]{2,1,0:T(8,128)(2,1)} %spread.2.m_ref, bf16[6,2,384,384]{3,2,1,0:T(8,128)(2,1)} %bitcast.167, bf16[6,2,384,384]{3,2,1,0:T(8,128)(2,1)} %bitcast.168, ...), custom_call_target="tpu_custom_call", output_to_operand_aliasing={{}: (5, {})} | custom-call | flops 3623878656 | bytes 48000000 | tf_op jit(solution)/shard_map/forward/pallas_call | solution.py:187
  361.6 13.1 %backward.4 = (bf16[16,384,1024]{2,1,0:T(8,128)(2,1)}, bf16[4,2,4,96,384]{4,3,2,1,0:T(8,128)(2,1)}) custom-call(s32[4]{0:T(128)} %get-tuple-element.184.at_ref, s32[4]{0:T(128)} %get-tuple-element.185.wat_ref, bf16[16,384,1024]{2,1,0:T(8,128)(2,1)} %spread.2.m_ref, bf16[16,384,1024]{2,1,0:T(8,128)(2,1)} %get-tuple-element.100.b_ref, ...), custom_call_target="tpu_custom_call", output_to_operand_aliasing={{0}: (3, {})} | custom-call | flops 6039797760 | bytes 60000000 | tf_op jit(solution)/shard_map/backward/pallas_call | solution.py:234
  382.7 18.0 %backward.5 = (bf16[16,384,1024]{2,1,0:T(8,128)(2,1)}, bf16[6,2,4,96,384]{4,3,2,1,0:T(8,128)(2,1)}) custom-call(s32[6]{0:T(128)} %stack.236.at_ref, s32[6]{0:T(128)} %iota.25.wat_ref, bf16[16,384,1024]{2,1,0:T(8,128)(2,1)} %spread.2.m_ref, bf16[16,384,1024]{2,1,0:T(8,128)(2,1)} %get-tuple-element.106.b_ref, ...), custom_call_target="tpu_custom_call", output_to_operand_aliasing={{0}: (3, {})} | custom-call | flops 9059696640 | bytes 90000000 | tf_op jit(solution)/shard_map/backward/pallas_call | solution.py:234
  403.1 6.5 collective-permute-start.24
  416.5 26.2 %gather.2 = (bf16[2,4,256,1536]{3,2,1,0:T(8,128)(2,1)}, bf16[2,4,256,1536]{3,2,1,0:T(8,128)(2,1)}, bf16[8,2,96,384]{3,2,1,0:T(8,128)(2,1)}) custom-call(s32[2]{0:T(128)} %pad_add_fusion.pos_ref, bf16[16,384,1024]{2,1,0:T(8,128)(2,1)} %get-tuple-element.113.mixed_ref, bf16[4,256,1536]{2,1,0:T(8,128)(2,1)} %all-to-all-done.refs_0_, ...), custom_call_target="tpu_custom_call" | custom-call | flops 2415919104 | bytes 76000000 | tf_op jit(solution)/shard_map/gather/pallas_call | solution.py:153
  453.1 11.0 %forward.5.mixed_ref = bf16[16,384,1024]{2,1,0:T(8,128)(2,1)} custom-call(s32[6]{0:T(128)} %stack.236.at_ref, s32[6]{0:T(128)} %iota.21.wat_ref, bf16[16,384,1024]{2,1,0:T(8,128)(2,1)} %spread.2.m_ref, bf16[6,2,384,384]{3,2,1,0:T(8,128)(2,1)} %bitcast.35.li_ref.ro_ref, ...), custom_call_target="tpu_custom_call", output_to_operand_aliasing={{}: (5, {})} | custom-call | flops 3623878656 | bytes 48000000 | tf_op jit(solution)/shard_map/forward/pallas_call | solution.py:187
  464.1 8.6 %collective-permute-done.27 = bf16[16,96,384]{2,1,0:T(8,128)(2,1)} collective-permute-done((bf16[16,96,384]{2,1,0:T(8,128)(2,1)}, bf16[16,96,384]{2,1,0:T(8,128)(2,1)}, u32[]{:S(2)}, u32[]{:S(2)}) %collective-permute-start.27) | collective-permute-done | bytes 1179680 | tf_op jit(solution)/shard_map/ppermute | solution.py:265
  472.7 5.2 collective-permute-done.28
  487.6 26.6 %gather.3 = (bf16[2,4,256,1536]{3,2,1,0:T(8,128)(2,1)}, bf16[2,4,256,1536]{3,2,1,0:T(8,128)(2,1)}, bf16[8,2,96,384]{3,2,1,0:T(8,128)(2,1)}) custom-call(s32[2]{0:T(128)} %pad_add_fusion.pos_ref, bf16[16,384,1024]{2,1,0:T(8,128)(2,1)} %forward.5.mixed_ref, bf16[4,256,1536]{2,1,0:T(8,128)(2,1)} %all-to-all-done.1.refs_0_, ...), custom_call_target="tpu_custom_call" | custom-call | flops 2415919104 | bytes 76000000 | tf_op jit(solution)/shard_map/gather/pallas_call | solution.py:153
  514.2 15.4 %collective-permute-done.30 = bf16[16,96,384]{2,1,0:T(8,128)(2,1)S(1)} collective-permute-done((bf16[16,96,384]{2,1,0:T(8,128)(2,1)}, bf16[16,96,384]{2,1,0:T(8,128)(2,1)S(1)}, u32[]{:S(2)}, u32[]{:S(2)}) %collective-permute-start.30) | collective-permute-done | bytes 1179680 | tf_op jit(solution)/shard_map/ppermute | solution.py:265
  535.1 8.3 %collective-permute-start.32 = (bf16[16,96,384]{2,1,0:T(8,128)(2,1)}, bf16[16,96,384]{2,1,0:T(8,128)(2,1)S(1)}, u32[]{:S(2)}, u32[]{:S(2)}) collective-permute-start(bf16[16,96,384]{2,1,0:T(8,128)(2,1)} %add_convert_fusion.3), channel_id=1, source_target_pairs={{0,4},{4,8},{8,12},{1,5},{5,9},{9,13},{2,6},{6,10},{10,14},{3,7},{... | collective-permute-start | bytes 3538952 | tf_op jit(solution)/shard_map/ppermute | solution.py:265
  543.5 20.6 %collective-permute-done.33 = bf16[16,96,384]{2,1,0:T(8,128)(2,1)} collective-permute-done((bf16[16,96,384]{2,1,0:T(8,128)(2,1)}, bf16[16,96,384]{2,1,0:T(8,128)(2,1)}, u32[]{:S(2)}, u32[]{:S(2)}) %collective-permute-start.33) | collective-permute-done | bytes 1179680 | tf_op jit(solution)/shard_map/ppermute | solution.py:269
  566.9 7.1 fusion
  574.0 4.8 all-to-all-start.3
  578.8 5.4 fusion.3
  584.2 70.1 %collective-permute-done.35 = bf16[4,256,1536]{2,1,0:T(8,128)(2,1)} collective-permute-done((bf16[4,256,1536]{2,1,0:T(8,128)(2,1)}, bf16[4,256,1536]{2,1,0:T(8,128)(2,1)}, u32[]{:S(2)}, u32[]{:S(2)}) %collective-permute-start.35) | collective-permute-done | bytes 3145760 | tf_op jit(solution)/shard_map/ppermute | solution.py:257
  654.3 6.7 fusion.1
  661.0 7.7 %all-to-all-done.3 = bf16[4,256,1536]{2,1,0:T(8,128)(2,1)S(1)} async-done(((bf16[4,256,1536]{2,1,0:T(8,128)(2,1)}), bf16[4,256,1536]{2,1,0:T(8,128)(2,1)S(1)}, u32[]{:S(2)}, u32[]{:S(2)}) %all-to-all-start.3) | async-done | bytes 3145760 | tf_op jit(solution)/shard_map/all_to_all | solution.py:280
  685.2 10.1 %collective-permute-done.38 = bf16[2,384,384]{2,1,0:T(8,128)(2,1)} collective-permute-done((bf16[2,384,384]{2,1,0:T(8,128)(2,1)}, bf16[2,384,384]{2,1,0:T(8,128)(2,1)}, u32[]{:S(2)}, u32[]{:S(2)}) %collective-permute-start.38) | collective-permute-done | bytes 589856 | tf_op jit(solution)/shard_map/ppermute | solution.py:257
  697.9 14.3 %collective-permute-done.36 = bf16[2,192,384]{2,1,0:T(8,128)(2,1)S(1)} collective-permute-done((bf16[2,192,384]{2,1,0:T(8,128)(2,1)S(1)}, bf16[2,192,384]{2,1,0:T(8,128)(2,1)S(1)}, u32[]{:S(2)}, u32[]{:S(2)}) %collective-permute-start.36) | collective-permute-done | bytes 294944 | tf_op jit(solution)/shard_map/ppermute | solution.py:257
  (193 shorter events, 171.3 us)
Async XLA Ops:
  7.2 113.5 %all-to-all-start = ((bf16[4,256,1536]{2,1,0:T(8,128)(2,1)}), bf16[4,256,1536]{2,1,0:T(8,128)(2,1)}, u32[]{:S(2)}, u32[]{:S(2)}) async-start(bf16[4,256,1536]{2,1,0:T(8,128)(2,1)} %bitcast.190), calls=%async_computation | async-start | bytes 6291456 | tf_op jit(solution)/shard_map/all_to_all | solution.py:280
  16.8 56.0 %collective-permute-start = (bf16[8,2,96,96]{2,3,1,0:T(8,128)(2,1)S(1)}, bf16[8,2,96,96]{2,3,1,0:T(8,128)(2,1)S(1)}, u32[]{:S(2)}, u32[]{:S(2)}) collective-permute-start(bf16[8,2,96,96]{2,3,1,0:T(8,128)(2,1)S(1)} %constant_dynamic-slice_fusion.1), channel_id=1, source_target_pairs={{0,4},{4,8},{8,12},{1,5},{5,9},{9,13},{2,6},{6,10},{10,14},{3,7},{... | collective-permute-start | bytes 884744 | tf_op jit(solution)/shard_map/ppermute | solution.py:265
  20.7 55.6 %collective-permute-start.3 = (bf16[8,2,96,96]{2,3,1,0:T(8,128)(2,1)S(1)}, bf16[8,2,96,96]{2,3,1,0:T(8,128)(2,1)}, u32[]{:S(2)}, u32[]{:S(2)}) collective-permute-start(bf16[8,2,96,96]{2,3,1,0:T(8,128)(2,1)S(1)} %constant_dynamic-slice_fusion.1), channel_id=1, source_target_pairs={{12,8},{8,4},{4,0},{13,9},{9,5},{5,1},{14,10},{10,6},{6,2},{15,11}... | collective-permute-start | bytes 884744 | tf_op jit(solution)/shard_map/ppermute | solution.py:269
  76.3 32.1 %collective-permute-start.4 = (bf16[8,2,96,96]{2,3,1,0:T(8,128)(2,1)}, bf16[8,2,96,96]{2,3,1,0:T(8,128)(2,1)}, u32[]{:S(2)}, u32[]{:S(2)}) collective-permute-start(bf16[8,2,96,96]{2,3,1,0:T(8,128)(2,1)} %collective-permute-done.3), channel_id=1, source_target_pairs={{8,4},{4,0},{9,5},{5,1},{10,6},{6,2},{11,7},{7,3},{24,20},{20,16},... | collective-permute-start | bytes 884744 | tf_op jit(solution)/shard_map/ppermute | solution.py:269
  79.9 30.9 %collective-permute-start.2 = (bf16[8,2,96,96]{2,3,1,0:T(8,128)(2,1)}, bf16[8,2,96,96]{2,3,1,0:T(8,128)(2,1)}, u32[]{:S(2)}, u32[]{:S(2)}) collective-permute-start(bf16[8,2,96,96]{2,3,1,0:T(8,128)(2,1)} %collective-permute-done.1), channel_id=1, source_target_pairs={{8,12},{9,13},{10,14},{11,15},{24,28},{25,29},{26,30},{27,31}} | collective-permute-start | bytes 884744 | tf_op jit(solution)/shard_map/ppermute | solution.py:265
  120.7 106.2 %all-to-all-start.1 = ((bf16[4,256,1536]{2,1,0:T(8,128)(2,1)}), bf16[4,256,1536]{2,1,0:T(8,128)(2,1)}, u32[]{:S(2)}, u32[]{:S(2)}) async-start(bf16[4,256,1536]{2,1,0:T(8,128)(2,1)} %bitcast.191), calls=%async_computation.1 | async-start | bytes 6291456 | tf_op jit(solution)/shard_map/all_to_all | solution.py:280
  125.3 418.2 %reduce-scatter.3.cloned.1.call-start = ((), (), s32[]{:S(2)}) async-start(), calls=%async_computation.6 | async-start | bytes 1474560 | tf_op jit(solution)/shard_map/reduce_scatter | solution.py:390
  125.4 67.2 %collective-permute-start.11 = (bf16[4,256,1536]{2,1,0:T(8,128)(2,1)}, bf16[4,256,1536]{2,1,0:T(8,128)(2,1)}, u32[]{:S(2)}, u32[]{:S(2)}) collective-permute-start(bf16[4,256,1536]{2,1,0:T(8,128)(2,1)} %all-to-all-done.refs_0_), channel_id=1, source_target_pairs={{0,2},{2,0},{1,3},{3,1},{4,6},{6,4},{5,7},{7,5},{8,10},{10,8},{9,1... | collective-permute-start | bytes 9437192 | tf_op jit(solution)/shard_map/ppermute | solution.py:257
  126.9 113.8 %collective-permute-start.12 = (bf16[4,256,1536]{2,1,0:T(8,128)(2,1)}, bf16[4,256,1536]{2,1,0:T(8,128)(2,1)}, u32[]{:S(2)}, u32[]{:S(2)}) collective-permute-start(bf16[4,256,1536]{2,1,0:T(8,128)(2,1)} %all-to-all-done.refs_0_), channel_id=1, source_target_pairs={{0,1},{1,0},{2,3},{3,2},{4,5},{5,4},{6,7},{7,6},{8,9},{9,8},{10,11... | collective-permute-start | bytes 9437192 | tf_op jit(solution)/shard_map/ppermute | solution.py:257
  192.6 48.2 %collective-permute-start.13 = (bf16[4,256,1536]{2,1,0:T(8,128)(2,1)}, bf16[4,256,1536]{2,1,0:T(8,128)(2,1)}, u32[]{:S(2)}, u32[]{:S(2)}) collective-permute-start(bf16[4,256,1536]{2,1,0:T(8,128)(2,1)} %collective-permute-done.11.refs_1_), channel_id=1, source_target_pairs={{0,1},{1,0},{2,3},{3,2},{4,5},{5,4},{6,7},{7,6},{8,9},{9,8},{10,11... | collective-permute-start | bytes 9437192 | tf_op jit(solution)/shard_map/ppermute | solution.py:257
  192.7 33.2 %collective-permute-start.7 = (bf16[2,2,384,384]{3,2,1,0:T(8,128)(2,1)S(1)}, bf16[2,2,384,384]{3,2,1,0:T(8,128)(2,1)S(1)}, u32[]{:S(2)}, u32[]{:S(2)}) collective-permute-start(bf16[2,2,384,384]{3,2,1,0:T(8,128)(2,1)S(1)} %constant_dynamic-slice_fusion), channel_id=1, source_target_pairs={{0,4},{4,8},{8,12},{1,5},{5,9},{9,13},{2,6},{6,10},{10,14},{3,7},{... | collective-permute-start | bytes 3538952 | tf_op jit(solution)/shard_map/ppermute | solution.py:265
  196.4 30.5 %collective-permute-start.8 = (bf16[2,2,384,384]{3,2,1,0:T(8,128)(2,1)S(1)}, bf16[2,2,384,384]{3,2,1,0:T(8,128)(2,1)}, u32[]{:S(2)}, u32[]{:S(2)}) collective-permute-start(bf16[2,2,384,384]{3,2,1,0:T(8,128)(2,1)S(1)} %constant_dynamic-slice_fusion), channel_id=1, source_target_pairs={{12,8},{8,4},{4,0},{13,9},{9,5},{5,1},{14,10},{10,6},{6,2},{15,11}... | collective-permute-start | bytes 3538952 | tf_op jit(solution)/shard_map/ppermute | solution.py:269
  226.9 69.8 %collective-permute-start.14 = (bf16[4,256,1536]{2,1,0:T(8,128)(2,1)}, bf16[4,256,1536]{2,1,0:T(8,128)(2,1)}, u32[]{:S(2)}, u32[]{:S(2)}) collective-permute-start(bf16[4,256,1536]{2,1,0:T(8,128)(2,1)} %all-to-all-done.1.refs_0_), channel_id=1, source_target_pairs={{0,2},{2,0},{1,3},{3,1},{4,6},{6,4},{5,7},{7,5},{8,10},{10,8},{9,1... | collective-permute-start | bytes 9437192 | tf_op jit(solution)/shard_map/ppermute | solution.py:257
  228.4 30.3 %collective-permute-start.10 = (bf16[2,2,384,384]{3,2,1,0:T(8,128)(2,1)}, bf16[2,2,384,384]{3,2,1,0:T(8,128)(2,1)}, u32[]{:S(2)}, u32[]{:S(2)}) collective-permute-start(bf16[2,2,384,384]{3,2,1,0:T(8,128)(2,1)} %collective-permute-done.8), channel_id=1, source_target_pairs={{8,4},{4,0},{9,5},{5,1},{10,6},{6,2},{11,7},{7,3},{24,20},{20,16},... | collective-permute-start | bytes 3538952 | tf_op jit(solution)/shard_map/ppermute | solution.py:269
  259.5 33.2 %collective-permute-start.16 = (bf16[2,2,384,384]{3,2,1,0:T(8,128)(2,1)}, bf16[2,2,384,384]{3,2,1,0:T(8,128)(2,1)S(1)}, u32[]{:S(2)}, u32[]{:S(2)}) collective-permute-start(bf16[2,2,384,384]{3,2,1,0:T(8,128)(2,1)} %collective-permute-done.10), channel_id=1, source_target_pairs={{4,0},{5,1},{6,2},{7,3},{20,16},{21,17},{22,18},{23,19}} | collective-permute-start | bytes 3538952 | tf_op jit(solution)/shard_map/ppermute | solution.py:269
  261.7 41.1 %collective-permute-start.18 = (bf16[4,256,1536]{2,1,0:T(8,128)(2,1)}, bf16[4,256,1536]{2,1,0:T(8,128)(2,1)}, u32[]{:S(2)}, u32[]{:S(2)}) collective-permute-start(bf16[4,256,1536]{2,1,0:T(8,128)(2,1)} %all-to-all-done.1.refs_0_), channel_id=1, source_target_pairs={{0,1},{1,0},{2,3},{3,2},{4,5},{5,4},{6,7},{7,6},{8,9},{9,8},{10,11... | collective-permute-start | bytes 9437192 | tf_op jit(solution)/shard_map/ppermute | solution.py:257
  300.5 81.7 %collective-permute-start.17 = (bf16[3,2,2,384,384]{4,3,2,1,0:T(8,128)(2,1)S(1)}, bf16[3,2,2,384,384]{4,3,2,1,0:T(8,128)(2,1)}, u32[]{:S(2)}, u32[]{:S(2)}) collective-permute-start(bf16[3,2,2,384,384]{4,3,2,1,0:T(8,128)(2,1)S(1)} %pad_maximum_fusion), channel_id=1, source_target_pairs={{0,16},{16,0},{1,17},{17,1},{2,18},{18,2},{3,19},{19,3},{4,20},{20... | collective-permute-start | bytes 10616840 | tf_op jit(solution)/shard_map/ppermute | solution.py:257
  343.0 31.7 %collective-permute-start.20 = (bf16[16,96,384]{2,1,0:T(8,128)(2,1)}, bf16[16,96,384]{2,1,0:T(8,128)(2,1)}, u32[]{:S(2)}, u32[]{:S(2)}) collective-permute-start(bf16[16,96,384]{2,1,0:T(8,128)(2,1)} %bitcast.43), channel_id=1, source_target_pairs={{0,4},{1,5},{2,6},{3,7},{16,20},{17,21},{18,22},{19,23}} | collective-permute-start | bytes 3538952 | tf_op jit(solution)/shard_map/ppermute | solution.py:265
  378.3 32.9 %collective-permute-start.22 = (bf16[16,96,384]{2,1,0:T(8,128)(2,1)}, bf16[16,96,384]{2,1,0:T(8,128)(2,1)S(1)}, u32[]{:S(2)}, u32[]{:S(2)}) collective-permute-start(bf16[16,96,384]{2,1,0:T(8,128)(2,1)} %get-tuple-element.108), channel_id=1, source_target_pairs={{0,4},{4,8},{1,5},{5,9},{2,6},{6,10},{3,7},{7,11},{16,20},{20,24},... | collective-permute-start | bytes 3538952 | tf_op jit(solution)/shard_map/ppermute | solution.py:265
  403.1 39.6 %collective-permute-start.24 = (bf16[16,96,384]{2,1,0:T(8,128)(2,1)S(1)}, bf16[16,96,384]{2,1,0:T(8,128)(2,1)}, u32[]{:S(2)}, u32[]{:S(2)}) collective-permute-start(bf16[16,96,384]{2,1,0:T(8,128)(2,1)S(1)} %bitcast.182), channel_id=1, source_target_pairs={{0,4},{1,5},{2,6},{3,7},{16,20},{17,21},{18,22},{19,23}} | collective-permute-start | bytes 3538952 | tf_op jit(solution)/shard_map/ppermute | solution.py:265
  409.6 33.1 %collective-permute-start.25 = (bf16[16,96,384]{2,1,0:T(8,128)(2,1)S(1)}, bf16[16,96,384]{2,1,0:T(8,128)(2,1)}, u32[]{:S(2)}, u32[]{:S(2)}) collective-permute-start(bf16[16,96,384]{2,1,0:T(8,128)(2,1)S(1)} %bitcast.181), channel_id=1, source_target_pairs={{12,8},{13,9},{14,10},{15,11},{28,24},{29,25},{30,26},{31,27}} | collective-permute-start | bytes 3538952 | tf_op jit(solution)/shard_map/ppermute | solution.py:269
  442.7 35.1 %collective-permute-start.26 = (bf16[2,4,256,1536]{3,2,1,0:T(8,128)(2,1)}, bf16[2,4,256,1536]{3,2,1,0:T(8,128)(2,1)}, u32[]{:S(2)}, u32[]{:S(2)}) collective-permute-start(bf16[2,4,256,1536]{3,2,1,0:T(8,128)(2,1)} %get-tuple-element.121), channel_id=1, source_target_pairs={{0,1},{1,0},{2,3},{3,2},{4,5},{5,4},{6,7},{7,6},{8,9},{9,8},{10,11... | collective-permute-start | bytes 18874376 | tf_op jit(solution)/shard_map/ppermute | solution.py:257
  482.2 84.6 %collective-permute-start.29 = (bf16[4,256,1536]{2,1,0:T(8,128)(2,1)}, bf16[4,256,1536]{2,1,0:T(8,128)(2,1)}, u32[]{:S(2)}, u32[]{:S(2)}) collective-permute-start(bf16[4,256,1536]{2,1,0:T(8,128)(2,1)} %fusion.2), channel_id=1, source_target_pairs={{0,2},{2,0},{1,3},{3,1},{4,6},{6,4},{5,7},{7,5},{8,10},{10,8},{9,1... | collective-permute-start | bytes 9437192 | tf_op jit(solution)/shard_map/ppermute | solution.py:257
  483.7 45.9 %collective-permute-start.30 = (bf16[16,96,384]{2,1,0:T(8,128)(2,1)}, bf16[16,96,384]{2,1,0:T(8,128)(2,1)S(1)}, u32[]{:S(2)}, u32[]{:S(2)}) collective-permute-start(bf16[16,96,384]{2,1,0:T(8,128)(2,1)} %get-tuple-element.131), channel_id=1, source_target_pairs={{0,4},{4,8},{1,5},{5,9},{2,6},{6,10},{3,7},{7,11},{16,20},{20,24},... | collective-permute-start | bytes 3538952 | tf_op jit(solution)/shard_map/ppermute | solution.py:265
  485.8 43.8 %collective-permute-start.31 = (bf16[16,96,384]{2,1,0:T(8,128)(2,1)}, bf16[16,96,384]{2,1,0:T(8,128)(2,1)}, u32[]{:S(2)}, u32[]{:S(2)}) collective-permute-start(bf16[16,96,384]{2,1,0:T(8,128)(2,1)} %get-tuple-element.132), channel_id=1, source_target_pairs={{12,8},{8,4},{13,9},{9,5},{14,10},{10,6},{15,11},{11,7},{28,24},{2... | collective-permute-start | bytes 3538952 | tf_op jit(solution)/shard_map/ppermute | solution.py:269
  532.2 31.9 %collective-permute-start.33 = (bf16[16,96,384]{2,1,0:T(8,128)(2,1)}, bf16[16,96,384]{2,1,0:T(8,128)(2,1)}, u32[]{:S(2)}, u32[]{:S(2)}) collective-permute-start(bf16[16,96,384]{2,1,0:T(8,128)(2,1)} %add_convert_fusion.2), channel_id=1, source_target_pairs={{12,8},{8,4},{4,0},{13,9},{9,5},{5,1},{14,10},{10,6},{6,2},{15,11}... | collective-permute-start | bytes 3538952 | tf_op jit(solution)/shard_map/ppermute | solution.py:269
  535.1 31.7 %collective-permute-start.32 = (bf16[16,96,384]{2,1,0:T(8,128)(2,1)}, bf16[16,96,384]{2,1,0:T(8,128)(2,1)S(1)}, u32[]{:S(2)}, u32[]{:S(2)}) collective-permute-start(bf16[16,96,384]{2,1,0:T(8,128)(2,1)} %add_convert_fusion.3), channel_id=1, source_target_pairs={{0,4},{4,8},{8,12},{1,5},{5,9},{9,13},{2,6},{6,10},{10,14},{3,7},{... | collective-permute-start | bytes 3538952 | tf_op jit(solution)/shard_map/ppermute | solution.py:265
  574.0 94.8 %all-to-all-start.3 = ((bf16[4,256,1536]{2,1,0:T(8,128)(2,1)}), bf16[4,256,1536]{2,1,0:T(8,128)(2,1)S(1)}, u32[]{:S(2)}, u32[]{:S(2)}) async-start(bf16[4,256,1536]{2,1,0:T(8,128)(2,1)} %fusion), calls=%async_computation.4 | async-start | bytes 6291456 | tf_op jit(solution)/shard_map/all_to_all | solution.py:280
  578.8 104.9 %reduce-scatter.5.cloned.1.call-start = ((), (), s32[]{:S(2)}) async-start(), calls=%async_computation.7 | async-start | bytes 1474560 | tf_op jit(solution)/shard_map/reduce_scatter | solution.py:406
  584.2 70.1 %collective-permute-start.35 = (bf16[4,256,1536]{2,1,0:T(8,128)(2,1)}, bf16[4,256,1536]{2,1,0:T(8,128)(2,1)}, u32[]{:S(2)}, u32[]{:S(2)}) collective-permute-start(bf16[4,256,1536]{2,1,0:T(8,128)(2,1)} %fusion.3), channel_id=1, source_target_pairs={{0,2},{2,0},{1,3},{3,1},{4,6},{6,4},{5,7},{7,5},{8,10},{10,8},{9,1... | collective-permute-start | bytes 9437192 | tf_op jit(solution)/shard_map/ppermute | solution.py:257
  668.7 75.0 %all-to-all-start.2 = ((bf16[4,256,1536]{2,1,0:T(8,128)(2,1)}), bf16[4,256,1536]{2,1,0:T(8,128)(2,1)}, u32[]{:S(2)}, u32[]{:S(2)}) async-start(bf16[4,256,1536]{2,1,0:T(8,128)(2,1)} %fusion.1), calls=%async_computation.3 | async-start | bytes 6291456 | tf_op jit(solution)/shard_map/all_to_all | solution.py:280
  681.8 31.3 %collective-permute-start.40 = (bf16[2,384,384]{2,1,0:T(8,128)(2,1)}, bf16[2,384,384]{2,1,0:T(8,128)(2,1)}, u32[]{:S(2)}, u32[]{:S(2)}) collective-permute-start(bf16[2,384,384]{2,1,0:T(8,128)(2,1)} %get-tuple-element.173), channel_id=1, source_target_pairs={{0,2},{2,0},{1,3},{3,1},{4,6},{6,4},{5,7},{7,5},{8,10},{10,8},{9,1... | collective-permute-start | bytes 1769480 | tf_op jit(solution)/shard_map/ppermute | solution.py:257
  (37 other events, 786.1 us)
Sparse Core Ops, SparseCore 0:
  487.7 45.7 reduce-scatter.2
  584.3 52.0 reduce-scatter.4
